TPU v7x, 512 devices: a whole 4x8x8 slice. The times are simulated.
512 devices in a mesh: enc: 16 (over y, core), seq: 32 (over z, x).
Axes of the slice: x: 4, y: 8, z: 8, core: 2. Of those that a mesh axis runs over, the one named last changes fastest.
Arguments:
- clip_features: bfloat16 [16, 32, 4, 16, 16, 512], P('enc', 'seq'), may hold values from -6 to 6
- clip_shape: int32 [16, 32, 3], P('enc', 'seq'), may hold values from 0 to 16, as said below
- packing: int32 [16, 32, 2, 2], P('enc', 'seq'), may hold values from -1 to 15, as said below
- conv_weight: bfloat16 [27, 16, 512], replicated, may hold values from -0.0546875 to 0.0546875
- embed_weight: bfloat16 [64, 2048], replicated, may hold values from -0.75 to 0.75
- mod_shift: float32 [2048], replicated, may hold values from -3 to 3
- mod_scale: float32 [2048], replicated, may hold values from -2 to 2
- qkv_weight: bfloat16 [3, 2048, 2048], P(None, 'seq', 'enc'), may hold values from -0.125 to 0.125
- q_gain: float32 [128], replicated, may hold values from 0.9 to 1.8
- k_gain: float32 [128], replicated, may hold values from 0.9 to 1.8
Outputs:
- attended: bfloat16 [32, 2048, 2048], P('seq', 'enc')
Inputs may be any that keep to these rules, and one draw needn't show every extreme that they name: `clip_shape`: Frames, height and width of each device's clip in latent pixels; height and width are even and at least 2, frames at most 4, height at most 16, width at most 16, and frames * height * width / 4 at most 256. Frames is 0 on some devices of every seq index; in every draw some device of each seq index has a clip of 4 x 16 x 16. `packing`: for each block slot: the enc index that owns it in its buffer and its block offset there, below the number of enc devices and below 1; both are -1 exactly for the slots past a clip's last token. Among the devices of one seq index no two blocks name the same owner and offset.
All inputs are finite; a program needn't handle non-finite values.
Results may differ from a plain program's by a relative error of at most 0.0075.
Values may be sent and summed in bfloat16 or wider, within the bound.
A program may use at most 128 MiB of HBM per device.

v0:
```python
import jax
import jax.numpy as jnp
from jax import lax
from jax.sharding import PartitionSpec as P

BLOCK = 128
ROWS = 128
NBS = 2


eps_norm = 1e-06


def encode(features, clip_dims, conv_weight):
    frames_cap, height_cap, width_cap, feat_count = features.shape
    half_h = height_cap // 2
    half_w = width_cap // 2
    latent_ch = conv_weight.shape[1]
    frame_ix = jnp.arange(frames_cap)[:, None, None]
    row_ix = jnp.arange(height_cap)[None, :, None]
    col_ix = jnp.arange(width_cap)[None, None, :]
    inside = (frame_ix < clip_dims[0]) & (row_ix < clip_dims[1]) & (col_ix < clip_dims[2])
    masked = jnp.where(inside[..., None], features, jnp.zeros_like(features))
    padded = jnp.pad(masked, ((2, 0), (1, 1), (1, 1), (0, 0)))
    summed = jnp.zeros((latent_ch, frames_cap * height_cap * width_cap), jnp.float32)
    for tap_depth in range(3):
        for tap_row in range(3):
            for tap_col in range(3):
                shifted = padded[
                    tap_depth : tap_depth + frames_cap,
                    tap_row : tap_row + height_cap,
                    tap_col : tap_col + width_cap,
                ]
                shifted = shifted.reshape(-1, feat_count)
                summed = summed + lax.dot_general(
                    conv_weight[9 * tap_depth + 3 * tap_row + tap_col],
                    shifted,
                    (((1,), (1,)), ((), ())),
                    preferred_element_type=jnp.float32,
                )
    latent_map = summed.astype(jnp.bfloat16).reshape(latent_ch, frames_cap, half_h, 2, half_w, 2)
    patches = latent_map.transpose(0, 3, 5, 1, 2, 4).reshape(
        4 * latent_ch, frames_cap * half_h * half_w
    )
    clip_h = clip_dims[1] // 2
    clip_w = clip_dims[2] // 2
    per_frame = clip_h * clip_w
    token_ix = jnp.arange(NBS * BLOCK)
    frame_of = token_ix // per_frame
    within = token_ix % per_frame
    grid_ix = frame_of * (half_h * half_w) + within // clip_w * half_w + within % clip_w
    is_live = token_ix < clip_dims[0] * per_frame
    grid_ix = jnp.where(is_live, grid_ix, 0)
    tokens = jnp.where(
        is_live[None, :], jnp.take(patches, grid_ix, axis=1), jnp.zeros((), jnp.bfloat16)
    )
    blocks = tokens.reshape(4 * latent_ch, NBS, BLOCK).transpose(1, 0, 2)
    counts = jnp.clip(clip_dims[0] * per_frame - jnp.arange(NBS) * BLOCK, 0, BLOCK)
    return (blocks, counts)


def qk_norm(projected, scale_gain, head_dim):
    per_head = projected.reshape(projected.shape[0], -1, head_dim)
    normed = (
        per_head
        * lax.rsqrt(jnp.mean(per_head * per_head, -1, keepdims=True) + eps_norm)
        * scale_gain
    )
    return normed.astype(jnp.bfloat16).reshape(projected.shape)


def norm_project(embedded, mod_shift, mod_scale, weights, q_gain, k_gain):
    head_dim = q_gain.shape[0]
    widened = embedded.astype(jnp.float32)
    row_mean = jnp.mean(widened, -1, keepdims=True)
    centered = widened - row_mean
    row_var = jnp.mean(centered * centered, -1, keepdims=True)
    normed_rows = (centered * lax.rsqrt(row_var + eps_norm) * (1.0 + mod_scale) + mod_shift).astype(
        jnp.bfloat16
    )
    query_raw = jnp.dot(normed_rows, weights[0], preferred_element_type=jnp.float32)
    key_raw = jnp.dot(normed_rows, weights[1], preferred_element_type=jnp.float32)
    value_raw = jnp.dot(normed_rows, weights[2], preferred_element_type=jnp.float32)
    return (
        qk_norm(query_raw, q_gain, head_dim),
        qk_norm(key_raw, k_gain, head_dim),
        value_raw.astype(jnp.bfloat16),
    )


def attend(query_rows, key_rows, value_rows, seg_rows, head_dim):
    row_count = query_rows.shape[0]
    heads_here = query_rows.shape[1] // head_dim
    block_rows = 512
    query_blocks = query_rows.reshape(row_count // block_rows, block_rows, heads_here, head_dim)
    seg_blocks = seg_rows.reshape(row_count // block_rows, block_rows)
    key_heads = key_rows.reshape(row_count, heads_here, head_dim)
    value_heads = value_rows.reshape(row_count, heads_here, head_dim)

    def one_block(inputs):
        query_block, seg_block = inputs
        scores = jnp.einsum(
            "qhd,khd->hqk", query_block, key_heads, preferred_element_type=jnp.float32
        ) * head_dim ** (-0.5)
        same_seg = seg_block[:, None] == seg_rows[None, :]
        exp_scores = jnp.where(same_seg[None], jnp.exp(scores), 0.0)
        attn_weights = (exp_scores / jnp.sum(exp_scores, -1, keepdims=True)).astype(jnp.bfloat16)
        mixed = jnp.einsum(
            "hqk,khd->qhd", attn_weights, value_heads, preferred_element_type=jnp.float32
        )
        return mixed.astype(jnp.bfloat16).reshape(block_rows, heads_here * head_dim)

    return lax.map(one_block, (query_blocks, seg_blocks)).reshape(row_count, heads_here * head_dim)


def on_device(
    clip_features,
    clip_shape,
    packing,
    conv_weight,
    embed_weight,
    mod_shift,
    mod_scale,
    qkv_weight,
    q_gain,
    k_gain,
):
    head_dim = q_gain.shape[0]
    blocks, counts = encode(clip_features[0, 0], clip_shape[0, 0], conv_weight)
    plan_rows = packing[0, 0]
    own_blocks = ROWS // BLOCK
    part_blocks = lax.all_gather(blocks, "enc", axis=0, tiled=True)
    part_plan = lax.all_gather(plan_rows, "enc", axis=0, tiled=True)
    part_counts = lax.all_gather(counts, "enc", axis=0, tiled=True)
    my_index = lax.axis_index("enc")
    item_count = part_blocks.shape[0]
    source = jnp.arange(item_count) // NBS
    offset_ix = jnp.arange(own_blocks)[:, None]
    selector = (part_plan[None, :, 0] == my_index) & (part_plan[None, :, 1] == offset_ix)
    moved_in = jnp.einsum(
        "oj,jfb->ofb",
        selector.astype(jnp.bfloat16),
        part_blocks,
        preferred_element_type=jnp.float32,
    )
    seg_ids = jnp.sum(jnp.where(selector, source[None, :] + 1, 0), 1)
    live_rows = jnp.sum(jnp.where(selector, part_counts[None, :], 0), 1)
    meta_info = jnp.stack([seg_ids, live_rows], -1).astype(jnp.int32)
    latent_buf = moved_in.astype(jnp.bfloat16)
    position = jnp.arange(BLOCK)[None, :]
    seg_own = jnp.where(position < meta_info[:, 1:2], meta_info[:, 0:1], 0)
    weights = lax.all_gather(qkv_weight, "seq", axis=1, tiled=True)
    summed = jnp.einsum("ofb,fd->obd", latent_buf, embed_weight, preferred_element_type=jnp.float32)
    embedded_own = summed.reshape(-1, embed_weight.shape[1]).astype(jnp.bfloat16)
    rows_part, seg_part = lax.all_gather(
        (embedded_own, seg_own.reshape(-1)), "enc", axis=0, tiled=True
    )
    row_count = rows_part.shape[0]
    mapped = lax.map(
        lambda row_block: norm_project(row_block, mod_shift, mod_scale, weights, q_gain, k_gain),
        rows_part.reshape(row_count // 512, 512, rows_part.shape[1]),
    )
    query_rows = mapped[0].reshape(row_count, -1)
    key_rows = mapped[1].reshape(row_count, -1)
    value_rows = mapped[2].reshape(row_count, -1)
    attended = attend(query_rows, key_rows, value_rows, seg_part, head_dim)
    regrouped = lax.all_to_all(attended, "enc", split_axis=0, concat_axis=1, tiled=True)
    return regrouped[None]


def solution(mesh):
    return jax.shard_map(
        on_device,
        mesh=mesh,
        in_specs=(
            P("enc", "seq", None, None, None, None),
            P("enc", "seq", None),
            P("enc", "seq", None, None),
            P(),
            P(),
            P(),
            P(),
            P(None, "seq", "enc"),
            P(),
            P(),
        ),
        out_specs=P("seq", "enc", None),
        check_vma=False,
    )
```

profile of v0, /device:TPU:1, one launch (start us, length us, event | category | flops | bytes accessed | tf_op | source)
XLA Modules:
  0.0 264.6 jit_solution(1787968237331632074)
XLA Ops:
  12.2 7.0 %pad_slice_fusion = (bf16[4,16,16,512]{3,2,1,0:T(8,128)(2,1)S(1)}, bf16[4,16,16,512]{3,2,1,0:T(8,128)(2,1)}, bf16[4,16,16,512]{3,2,1,0:T(8,128)(2,1)}, bf16[4,16...) fusion(bf16[4,16,16,512]{3,2,1,0:T(8,128)(2,1)S(1)} %bitcast_se, ...), kind=kLoop, calls=%fused_computation.48 | loop fusion | bytes 20971520 | tf_op jit(solution)/shard_map/slice | solution.py:29
  19.2 3.1 %pad_slice_fusion.1 = (bf16[4,16,16,512]{3,2,1,0:T(8,128)(2,1)}, bf16[4,16,16,512]{3,2,1,0:T(8,128)(2,1)S(1)}, bf16[4,16,16,512]{3,2,1,0:T(8,128)(2,1)S(1)}, bf1...) fusion(bf16[4,16,16,512]{3,2,1,0:T(8,128)(2,1)S(1)} %bitcast_se, ...), kind=kLoop, calls=%fused_computation.49 | loop fusion | bytes 8388608 | tf_op jit(solution)/shard_map/slice | solution.py:29
  48.8 20.9 %all-gather = s32[1,1,32,2]{3,1,0,2:T(1,128)S(1)} all-gather(s32[1,1,2,2]{3,1,0,2:T(1,128)S(1)} %bitcast.355), channel_id=2, replica_groups=mesh['enc'=16,'seq'=32] {'enc'}, dimensions={2}, use_global_device_ids=true | all-gather | bytes 272 | tf_op jit(solution)/shard_map/all_gather | solution.py:133
  71.8 10.6 %all-reduce.1 = s32[32]{0:T(128)S(1)} all-reduce(s32[32]{0:T(128)S(1)} %clamp_dynamic-update-slice_fusion), channel_id=1, replica_groups=mesh['enc'=16,'seq'=32] {'enc'}, use_global_device_ids=true, to_apply=%add.1 | all-reduce | flops 32 | bytes 256
  83.4 19.4 %all_gather.21 = bf16[32,64,128]{2,1,0:T(8,128)(2,1)S(1)} all-gather(bf16[2,64,128]{2,1,0:T(8,128)(2,1)S(1)} %select_bitcast_fusion), channel_id=1, replica_groups=mesh['enc'=16,'seq'=32] {'enc'}, dimensions={0}, use_global_device_ids=true | all-gather | bytes 557056 | tf_op jit(solution)/shard_map/all_gather | solution.py:132
  106.3 14.5 %all-gather.1 = s32[16,1,128]{2,1,0:T(1,128)S(1)} all-gather(s32[1,1,128]{2,1,0:T(1,128)S(1)} %fusion.105), channel_id=1, replica_groups=mesh['enc'=16,'seq'=32] {'enc'}, dimensions={0}, use_global_device_ids=true | all-gather | bytes 8704 | tf_op jit(solution)/shard_map/all_gather | solution.py:155
  122.2 39.8 %all-gather.5.cloned.1.call-done = bf16[2048,2048]{1,0:T(8,128)(2,1)} async-done(((bf16[128,2048]{1,0:T(8,128)(2,1)}), bf16[2048,2048]{1,0:T(8,128)(2,1)}) %all-gather.5.cloned.1.call-update) | async-done | bytes 8388624 | tf_op jit(solution)/shard_map/all_gather | solution.py:155
  162.9 55.6 %while.24 = (s32[]{:T(128)}, bf16[4,512,128]{1,2,0:T(8,128)(2,1)}, bf16[4,512,128]{2,1,0:T(8,128)(2,1)S(1)}, bf16[4,512,128]{2,1,0:T(8,128)(2,1)}, bf16[4,512,20...) while((s32[]{:T(128)}, bf16[4,512,128]{1,2,0:T(8,128)(2,1)}, ...), condition=%wide.region_5.6_spmd, body=%wide.region_0.5_spmd.sunk | while | flops 818613760 | bytes 18288764 | solution.py:159
  162.9 1.9 convert_reduce_fusion.2
  164.9 2.3 fusion.157
  167.2 2.4 fusion.158
  169.6 1.9 multiply_reduce_fusion.5
  174.4 2.4 fusion.161
  176.8 1.9 convert_reduce_fusion.2
  178.7 2.3 fusion.157
  181.0 2.4 fusion.158
  183.5 1.9 multiply_reduce_fusion.5
  188.3 2.4 fusion.161
  190.7 1.9 convert_reduce_fusion.2
  192.6 2.3 fusion.157
  194.9 2.4 fusion.158
  202.2 2.4 fusion.161
  204.6 1.9 convert_reduce_fusion.2
  206.5 2.3 fusion.157
  208.8 2.4 fusion.158
  216.1 2.4 fusion.161
  218.5 16.1 %while.25 = (s32[]{:T(128)}, bf16[4,512,128]{2,1,0:T(8,128)(2,1)S(1)}, s32[4,512]{1,0:T(4,128)S(1)}, s32[2048]{0:T(1024)S(1)}, bf16[4,512,1,128]{1,3,0,2:T(8,128...) while((s32[]{:T(128)}, bf16[4,512,128]{2,1,0:T(8,128)(2,1)S(1)}, ...), condition=%wide.region_10.11_spmd, body=%wide.region_8.10_spmd.sunk | while | flops 543227392 | bytes 9718365 | solution.py:113
  218.6 2.1 fusion.163
  222.6 2.1 fusion.163
  226.6 2.1 fusion.163
  230.6 2.1 fusion.163
  234.6 21.8 %all_to_all.16 = bf16[16,128,128]{2,1,0:T(8,128)(2,1)S(1)} all-to-all(bf16[16,128,128]{2,1,0:T(8,128)(2,1)S(1)} %bitcast.345), channel_id=1, replica_groups=mesh['enc'=16,'seq'=32] {'enc'}, dimensions={0} | all-to-all | bytes 1048576 | tf_op jit(solution)/shard_map/all_to_all | solution.py:167
  (168 shorter events, 58.5 us)
Async XLA Ops:
  6.5 96.7 %copy-start = (bf16[64,2048]{1,0:T(8,128)(2,1)S(1)}, bf16[64,2048]{1,0:T(8,128)(2,1)}, u32[]{:S(2)}) copy-start(bf16[64,2048]{1,0:T(8,128)(2,1)} %param.18) | copy-start | bytes 786436
  6.5 115.6 %all-gather.7.cloned.1.call-start = ((), (), s32[]{:S(2)}) async-start(), calls=%async_computation.2 | async-start | bytes 1622016 | tf_op jit(solution)/shard_map/all_gather | solution.py:152
  7.3 154.7 %all-gather.5.cloned.1.call-start = ((), (), s32[]{:S(2)}) async-start(), calls=%async_computation.1 | async-start | bytes 8912896 | tf_op jit(solution)/shard_map/all_gather | solution.py:155
  19.2 3.1 %copy-start.15 = (bf16[1,1,4,16,16,512]{5,4,3,2,1,0:T(8,128)(2,1)S(1)}, bf16[1,1,4,16,16,512]{5,4,3,2,1,0:T(8,128)(2,1)}, u32[]{:S(2)}) copy-start(bf16[1,1,4,16,16,512]{5,4,3,2,1,0:T(8,128)(2,1)} %param.14) | copy-start | bytes 3145732
  19.2 4.4 %copy-start.19 = (bf16[27,16,512]{2,1,0:T(8,128)(2,1)S(1)}, bf16[27,16,512]{2,1,0:T(8,128)(2,1)}, u32[]{:S(2)}) copy-start(bf16[27,16,512]{2,1,0:T(8,128)(2,1)} %param.17) | copy-start | bytes 1327108
  22.3 1.6 copy-start.14
  22.3 2.0 copy-start.13
  22.3 2.4 copy-start.12
  23.5 1.6 copy-start.11
  23.9 1.6 copy-start.10
  24.3 1.6 copy-start.9
  24.7 1.6 copy-start.8
  25.1 1.6 copy-start.7
  25.5 1.6 copy-start.6
  25.9 1.6 copy-start.5
  26.3 1.6 copy-start.4
  26.7 1.6 copy-start.3
  27.1 1.6 copy-start.2
  27.5 1.6 copy-start.1
  30.6 8.7 %copy-start.16 = (bf16[1,1,4,16,16,512]{5,4,3,2,1,0:T(8,128)(2,1)S(1)}, bf16[1,1,4,16,16,512]{5,4,3,2,1,0:T(8,128)(2,1)}, u32[]{:S(2)}) copy-start(bf16[1,1,4,16,16,512]{5,4,3,2,1,0:T(8,128)(2,1)} %broadcast_select_fusion) | copy-start | bytes 3145732
  31.8 11.4 %copy-start.17 = (bf16[4,16,16,512]{3,2,1,0:T(8,128)(2,1)S(1)}, bf16[4,16,16,512]{3,2,1,0:T(8,128)(2,1)}, u32[]{:S(2)}) copy-start(bf16[4,16,16,512]{3,2,1,0:T(8,128)(2,1)} %get-tuple-element.222) | copy-start | bytes 3145732
  37.6 4.4 %copy-start.18 = (bf16[4,16,16,512]{3,2,1,0:T(8,128)(2,1)S(1)}, bf16[4,16,16,512]{3,2,1,0:T(8,128)(2,1)}, u32[]{:S(2)}) copy-start(bf16[4,16,16,512]{3,2,1,0:T(8,128)(2,1)} %get-tuple-element.227) | copy-start | bytes 3145732
  42.1 6.7 %copy-start.24 = (s32[1,1,2,2]{3,2,1,0:T(2,128)S(1)}, s32[1,1,2,2]{3,2,1,0:T(2,128)}, u32[]{:S(2)}) copy-start(s32[1,1,2,2]{3,2,1,0:T(2,128)} %param.16) | copy-start | bytes 52
  45.6 117.3 %copy-start.20 = (f32[2048]{0:T(1024)S(1)}, f32[2048]{0:T(1024)}, u32[]{:S(2)}) copy-start(f32[2048]{0:T(1024)} %param.19) | copy-start | bytes 24580
  45.6 117.3 %copy-start.21 = (f32[2048]{0:T(1024)S(1)}, f32[2048]{0:T(1024)}, u32[]{:S(2)}) copy-start(f32[2048]{0:T(1024)} %param.20) | copy-start | bytes 24580
  45.6 117.3 %copy-start.22 = (f32[128]{0:T(128)S(1)}, f32[128]{0:T(128)}, u32[]{:S(2)}) copy-start(f32[128]{0:T(128)} %param.22) | copy-start | bytes 1540
  45.6 117.3 %copy-start.23 = (f32[128]{0:T(128)S(1)}, f32[128]{0:T(128)}, u32[]{:S(2)}) copy-start(f32[128]{0:T(128)} %param.23) | copy-start | bytes 1540
Sparse Core Ops, SparseCore 0:
  10.5 85.0 all-gather.6
  104.5 57.4 all-gather.4
where the time goes:
time: 266 us; the launch traced here: 265 us
  blocking collectives  87.3 us (33%)
  matrix products  58 us (22%)
  waiting for transfers between devices  40.5 us (15%)
  other arithmetic  38.9 us (15%)
  between operations  20.2 us (8%)
  local copies, waits for them, and re-layouts  19.3 us (7%)
    all_gather x1, waiting for transfers between devices, on_device(): lax.all_gather((embedded_own, seg_own.reshape(-1)), 'enc', axis=0, tiled=...  39.8 us
    all_to_all x1, blocking collectives, on_device(): lax.all_to_all(attended, 'enc', split_axis=0, concat_axis=1, tiled=True)  21.8 us
    all_gather x1, blocking collectives, on_device(): part_plan = lax.all_gather(plan_rows, 'enc', axis=0, tiled=True)  20.9 us
    all_gather x1, blocking collectives, on_device(): part_blocks = lax.all_gather(blocks, 'enc', axis=0, tiled=True)  19.4 us
    dot_general x27, matrix products, encode(): lax.dot_general(conv_weight[9 * tap_depth + 3 * tap_row + tap_col], shift...  15.9 us
    all_gather x1, blocking collectives, on_device(): lax.all_gather((embedded_own, seg_own.reshape(-1)), 'enc', axis=0, tiled=...  14.5 us
    unnamed x1, blocking collectives  10.6 us
    slice x2, local copies, waits for them, and re-layouts, encode(): padded[tap_depth:tap_depth + frames_cap, tap_row:tap_row + height_cap, ta...  10.1 us
  transfers between devices with their start and end apart: 2, of which 1 were waited for; matrix products, arithmetic and copies ran while one was open for 16% of the time, Pallas kernels for 0%

commit v1 on v0

v1 whole, which is shorter than its diff:
```python
import functools
import math

import jax
import jax.numpy as jnp
from jax import lax
from jax.experimental import pallas as pl
from jax.experimental.pallas import tpu as pltpu
from jax.sharding import PartitionSpec as P

MESH = pl.DeviceIdType.MESH
F32 = jnp.float32
BF16 = jnp.bfloat16
EPS = 1e-06
LATF = 64
LAT = 16
TOK = 256
BLOCK = 128
FRAME = 256
FC = 4
HD = 128


def mod(a, n):
    return lax.rem(a, n)


def near_first(n):
    order = []
    for d in range(1, n // 2 + 1):
        order.append(d)
        if n - d != d:
            order.append(n - d)
    return order


def split_bf16(value, terms):
    parts = []
    for _ in range(terms):
        part = value.astype(BF16)
        parts.append(part)
        value = value - part.astype(F32)
    return parts


def nt_dot(a, b):
    return lax.dot_general(a, b, (((1,), (1,)), ((), ())), preferred_element_type=F32)


def partial_fold(s, embed_ref, scale_ref, shift_ref, w_ref):
    embed = embed_ref[...].astype(F32)
    mean = jnp.mean(embed, -1, keepdims=True)
    window = pl.ds(pl.multiple_of((s // 2) * 128, 128), 128)
    a_part = (embed_ref[:, window].astype(F32) - mean) * (1.0 + scale_ref[:, window])
    shift_rows = jnp.broadcast_to(shift_ref[:, window], (16, 128))
    lhs = jnp.concatenate([a_part, shift_rows], 0)
    hi, lo = split_bf16(lhs, 2)
    lhs2 = jnp.concatenate([hi, lo], 1)
    half = lax.broadcasted_iota(jnp.int32, (128, 3 * HD), 0) // 64
    w_all = jnp.concatenate([w_ref[0], w_ref[1], w_ref[2]], 1).astype(F32)
    w_two = jnp.concatenate([w_all, w_all], 0)
    w_pad = jnp.where(half == mod(s, 2), w_two, 0.0).astype(BF16)
    rhs = jnp.concatenate([w_pad, w_pad], 0)
    return jnp.dot(lhs2, rhs, preferred_element_type=F32)


def token_places(frames, height, width):
    slot = lax.broadcasted_iota(jnp.int32, (1, TOK), 1).astype(F32)
    zero = jnp.zeros((1, TOK), jnp.int32)
    frames_v = (zero + frames).astype(F32)
    half_h = (zero + height).astype(F32) * 0.5
    half_w = (zero + width).astype(F32) * 0.5
    per_frame = half_h * half_w
    t = jnp.floor((slot + 0.5) / per_frame)
    within = slot - t * per_frame
    r = jnp.floor((within + 0.5) / half_w)
    q = within - r * half_w
    count = frames_v * per_frame
    return jnp.where(slot < count, t * FRAME + r * 32.0 + q * 2.0, -1.0), count


def clip_tokens(frames, height, width, feat_ref, conv_ref):
    lane = lax.broadcasted_iota(jnp.int32, (1, FRAME), 1)
    row, col = lane // 16, lane % 16
    inside = (row < height) & (col < width)
    conv = conv_ref[...]
    places, count = token_places(frames, height, width)
    spot = lax.broadcasted_iota(jnp.int32, (FRAME, TOK), 0).astype(F32)
    products = []
    tokens = jnp.zeros((LATF, TOK), F32)
    taps = 9 * LAT
    for t in range(FC):
        here = nt_dot(conv, feat_ref[t * FRAME : (t + 1) * FRAME, :])
        keep = inside & (lane < jnp.where(t < frames, FRAME, 0))
        products.append(jnp.where(keep, here, 0.0))
        summed = products[t][2 * taps :]
        if t >= 1:
            summed = summed + products[t - 1][taps : 2 * taps]
        if t >= 2:
            summed = summed + products[t - 2][:taps]
        third = 3 * LAT
        rows = summed[third : 2 * third]
        rows = rows + jnp.where(row >= 1, pltpu.roll(summed[:third], 16, 1), 0.0)
        rows = rows + jnp.where(row <= 14, pltpu.roll(summed[2 * third :], FRAME - 16, 1), 0.0)
        latent = rows[LAT : 2 * LAT]
        latent = latent + jnp.where(col >= 1, pltpu.roll(rows[:LAT], 1, 1), 0.0)
        latent = latent + jnp.where(col <= 14, pltpu.roll(rows[2 * LAT :], FRAME - 1, 1), 0.0)
        latent = latent.astype(BF16).astype(F32)
        phases = [latent] + [pltpu.roll(latent, FRAME - d, 1) for d in (1, 16, 17)]
        phases = jnp.concatenate(phases, 0).astype(BF16)
        pick = jnp.where(spot + float(t * FRAME) == places, 1.0, 0.0).astype(BF16)
        tokens = tokens + jnp.dot(phases, pick, preferred_element_type=F32)
    out_row = lax.broadcasted_iota(jnp.int32, (LATF, LATF), 0)
    in_row = lax.broadcasted_iota(jnp.int32, (LATF, LATF), 1)
    swap = jnp.where(in_row == (out_row % 4) * LAT + out_row // 4, 1.0, 0.0).astype(BF16)
    tokens = jnp.dot(swap, tokens.astype(BF16), preferred_element_type=F32)
    return tokens.astype(BF16), count


def gram_terms(embed_ref):
    embed = embed_ref[...]
    features = embed.shape[1]
    both = nt_dot(embed, embed)
    wide = embed.astype(F32)
    mean_col = jnp.mean(wide, -1, keepdims=True)
    ones = jnp.ones((8, features), BF16)
    mean_row = nt_dot(ones, embed)[:1] * (1.0 / features)
    gram = both * (1.0 / features) - mean_col * mean_row
    return jnp.concatenate(split_bf16(gram, 3), 0)


def move_kernel(
    ny,
    nz,
    nx,
    dims_ref,
    plan_ref,
    feat_hbm,
    conv_ref,
    embed_ref,
    scale_ref,
    shift_ref,
    w_ref,
    xt_ref,
    xq_ref,
    rk_ref,
    rq_ref,
    same_ref,
    fold_ref,
    head_ref,
    feat_ref,
    stage,
    sum_in,
    own_sum,
    cross_in,
    x_all,
    feat_sem,
    send1,
    recv1,
    send2,
    recv2,
    send3,
    recv3,
    send4,
    recv4,
    send5,
    recv5,
    send6,
    recv6,
    send7,
    recv7,
):
    e = lax.axis_index("enc")
    s = lax.axis_index("seq")
    y, c = e // 2, mod(e, 2)
    z, x = s // nx, mod(s, nx)
    group = LATF // nz
    rows = 3 * group + 8

    def at_y(d):
        return {"enc": mod(y + d, ny) * 2 + c, "seq": s}

    def at_z(d):
        return {"enc": e, "seq": mod(z + d, nz) * nx + x}

    def at_x(d):
        return {"enc": e, "seq": z * nx + mod(x + d, nx)}

    sibling = {"enc": y * 2 + 1 - c, "seq": s}

    feat_copy = pltpu.make_async_copy(feat_hbm, feat_ref, feat_sem)
    feat_copy.start()

    barrier = pltpu.get_barrier_semaphore()
    peers = [at_z(d) for d in range(1, nz)] + [at_x(d) for d in range(1, nx)]
    peers += [at_y(d) for d in range(1, ny)] + [sibling]
    for peer in peers:
        pl.semaphore_signal(barrier, inc=1, device_id=peer, device_id_type=MESH)

    sends = []

    def send(src, dst, send_sem, recv_sem, peer):
        copy = pltpu.make_async_remote_copy(
            src_ref=src,
            dst_ref=dst,
            send_sem=send_sem,
            recv_sem=recv_sem,
            device_id=peer,
            device_id_type=MESH,
        )
        copy.start()
        sends.append(copy)
        return copy

    part = partial_fold(s, embed_ref, scale_ref, shift_ref, w_ref)
    row8 = lax.broadcasted_iota(jnp.int32, (8, HD), 0)
    bias = jnp.zeros((8, HD), F32)
    for j in range(3):
        bias = jnp.where(row8 == j, part[LATF : LATF + 8, j * HD : (j + 1) * HD], bias)
    for g in range(nz):
        for j in range(3):
            stage[g, j * group : (j + 1) * group, :] = part[
                g * group : (g + 1) * group, j * HD : (j + 1) * HD
            ]
        stage[g, 3 * group :, :] = bias

    pl.semaphore_wait(barrier, len(peers))

    first = [
        send(stage.at[mod(z + d, nz)], sum_in.at[d], send1.at[d], recv1.at[d], at_z(d))
        for d in near_first(nz)
    ]

    feat_copy.wait()
    frames, height, width = dims_ref[0], dims_ref[1], dims_ref[2]
    tokens, count = clip_tokens(frames, height, width, feat_ref, conv_ref)
    for b in range(2):
        for i in range(4):
            x_all[e, 4 * b + i] = tokens[16 * i : 16 * i + 16, b * BLOCK : (b + 1) * BLOCK]
    row16 = lax.broadcasted_iota(jnp.int32, (16, BLOCK), 0)
    owner0 = (jnp.zeros((16, BLOCK), jnp.int32) + plan_ref[0]).astype(F32)
    owner1 = (jnp.zeros((16, BLOCK), jnp.int32) + plan_ref[2]).astype(F32)
    meta = jnp.where(row16 == 0, owner0, jnp.where(row16 == 1, owner1, count[:, :BLOCK]))
    x_all[e, 8] = meta.astype(BF16)
    x_first = [
        send(x_all.at[e], x_all.at[e], send6.at[d], recv6.at[d], at_y(d)) for d in near_first(ny)
    ]
    x_own = send(x_all.at[e], x_all.at[e], send7.at[0], recv7.at[0], sibling)

    total = stage[z]
    for copy in first:
        copy.wait_recv()
    for d in range(1, nz):
        total = total + sum_in[d]
    own_sum[...] = total
    second = [
        send(own_sum, cross_in.at[d], send2.at[d], recv2.at[d], at_x(d)) for d in near_first(nx)
    ]
    gram = gram_terms(embed_ref)
    for copy in second:
        copy.wait_recv()
    for d in range(1, nx):
        total = total + cross_in[d]

    bias = total[3 * group :]
    bias_hi = bias.astype(BF16).astype(F32)
    tail = jnp.where(row8 < 3, bias_hi, pltpu.roll(bias - bias_hi, 3, 0))
    head_ref[c, y] = jnp.concatenate([total[: 3 * group], tail], 0).astype(BF16)
    third = [
        send(head_ref.at[c, y], head_ref.at[c, y], send3.at[d], recv3.at[d], at_y(d))
        for d in near_first(ny)
    ]
    for copy in third:
        copy.wait_recv()

    def pack(core):
        whole = head_ref[core].astype(F32)[:, : 3 * group]
        fold_ref[core, z] = whole.reshape(ny * 3 * group, HD).astype(BF16)

    pack(c)
    fourth = [
        send(fold_ref.at[c, z], fold_ref.at[c, z], send4.at[d], recv4.at[d], at_z(d))
        for d in near_first(nz)
    ]
    fifth = [send(head_ref.at[c], head_ref.at[c], send5.at[0], recv5.at[0], sibling)]

    x_second = [x_own]
    for d, copy in zip(near_first(ny), x_first):
        copy.wait_recv()
        source = mod(y - d + ny, ny) * 2 + c
        x_second.append(
            send(x_all.at[source], x_all.at[source], send7.at[d], recv7.at[d], sibling)
        )
    for copy in x_second:
        copy.wait_recv()

    chosen = jnp.zeros((2, 4, 16, BLOCK), F32)
    is0 = jnp.zeros((1, BLOCK), F32)
    is1 = jnp.zeros((1, BLOCK), F32)
    live = jnp.zeros((1, BLOCK), F32)
    me = (jnp.zeros((1, BLOCK), jnp.int32) + e).astype(F32)
    for j in range(2 * ny):
        info = x_all[j, 8].astype(F32)
        here0 = jnp.where(info[0:1] == me, 1.0, 0.0)
        here1 = jnp.where(info[1:2] == me, 1.0, 0.0)
        here = here0 + here1
        is0, is1 = is0 + here0, is1 + here1
        live = live + here * info[2:3]
        chosen = chosen + x_all[j, 0:8].astype(F32).reshape(2, 4, 16, BLOCK) * here
    chosen = chosen.reshape(2, LATF, BLOCK)
    xt = jnp.concatenate([chosen[0].T, chosen[1].T], 0)
    xt16 = xt.astype(BF16)
    mixed = jnp.dot(
        jnp.concatenate([xt16, xt16, xt16], 1), gram, preferred_element_type=F32
    )
    var = jnp.sum(mixed * xt, -1, keepdims=True)
    rstd = jnp.broadcast_to(lax.rsqrt(jnp.maximum(var, 0.0) + EPS), (TOK, HD))
    xt_ref[...] = xt16
    xq_ref[...] = (chosen[0] * is0 + chosen[1] * is1).T.astype(BF16)
    rk_ref[...] = rstd
    rq_ref[...] = rstd[:BLOCK] * is0 + rstd[BLOCK:] * is1
    q_slot = lax.broadcasted_iota(jnp.int32, (BLOCK, BLOCK), 0).astype(F32) + is1 * BLOCK
    q_live = jnp.where(q_slot < live, 1.0, 0.0)
    for b in range(2):
        k_slot = lax.broadcasted_iota(jnp.int32, (1, BLOCK), 1).astype(F32) + float(b * BLOCK)
        k_live = jnp.where(k_slot < live, 1.0, 0.0)
        same_ref[:, b * BLOCK : (b + 1) * BLOCK] = jnp.where(q_live == k_live, 1.0, 0.0)

    for d, copy in zip(near_first(nz), fourth):
        copy.wait_recv()
        source = mod(z - d + nz, nz)
        fifth.append(
            send(
                fold_ref.at[c, source],
                fold_ref.at[c, source],
                send5.at[d],
                recv5.at[d],
                sibling,
            )
        )
    for copy in fifth:
        copy.wait_recv()
    pack(1 - c)
    for copy in sends:
        copy.wait_send()


def attend_kernel(
    ny, nz, xt_ref, xq_ref, rk_ref, rq_ref, same_ref, fold_ref, head_ref, qg_ref, kg_ref, out_ref
):
    group = LATF // nz
    xt, xq = xt_ref[...], xq_ref[...]
    rk, rq = rk_ref[...], rq_ref[...]
    same = same_ref[...]
    q_gain = qg_ref[...] * (HD ** -0.5 * math.log2(math.e))
    k_gain = kg_ref[...]
    ones = jnp.ones((TOK, HD), BF16)
    for core in range(2):
        for head in range(ny):
            start = head * 3 * group
            fold = fold_ref[core, :, start : start + 3 * group, :].astype(F32)
            fold = [
                fold[:, j * group : (j + 1) * group].reshape(LATF, HD).astype(BF16)
                for j in range(3)
            ]
            tail = head_ref[core, head].astype(F32)[3 * group :]
            bias = tail[0:3] + tail[3:6]
            q = jnp.dot(xq, fold[0], preferred_element_type=F32) * rq + bias[0:1]
            kv = jnp.dot(xt, jnp.concatenate(fold[1:], 1), preferred_element_type=F32)
            k = kv[:, :HD] * rk + bias[1:2]
            v = (kv[:, HD:] * rk + bias[2:3]).astype(BF16)
            q = q * lax.rsqrt(jnp.mean(q * q, -1, keepdims=True) + EPS) * q_gain
            k = k * lax.rsqrt(jnp.mean(k * k, -1, keepdims=True) + EPS) * k_gain
            scores = nt_dot(q.astype(BF16), k.astype(BF16))
            weights = (jnp.exp2(scores) * same).astype(BF16)
            mixed = jnp.dot(weights, jnp.concatenate([v, ones], 1), preferred_element_type=F32)
            column = (2 * head + core) * HD
            out_ref[:, column : column + HD] = (mixed[:, :HD] / mixed[:, HD:]).astype(BF16)


def whole(memory=pltpu.VMEM):
    return pl.BlockSpec(memory_space=memory)


def solution(mesh):
    ny = mesh.shape["enc"] // 2
    nx = 4 if mesh.shape["seq"] == 32 else 2
    nz = mesh.shape["seq"] // nx
    group = LATF // nz
    rows = 3 * group + 8
    dma = pltpu.SemaphoreType.DMA

    def on_device(
        clip_features,
        clip_shape,
        packing,
        conv_weight,
        embed_weight,
        mod_shift,
        mod_scale,
        qkv_weight,
        q_gain,
        k_gain,
    ):
        features = clip_features.shape[-1]
        moved = pl.pallas_call(
            functools.partial(move_kernel, ny, nz, nx),
            out_shape=(
                jax.ShapeDtypeStruct((TOK, LATF), BF16),
                jax.ShapeDtypeStruct((BLOCK, LATF), BF16),
                jax.ShapeDtypeStruct((TOK, HD), F32),
                jax.ShapeDtypeStruct((BLOCK, HD), F32),
                jax.ShapeDtypeStruct((BLOCK, TOK), F32),
                jax.ShapeDtypeStruct((2, nz, ny * 3 * group, HD), BF16),
                jax.ShapeDtypeStruct((2, ny, rows, HD), BF16),
            ),
            in_specs=[
                whole(pltpu.SMEM),
                whole(pltpu.SMEM),
                whole(pl.ANY),
                whole(),
                whole(),
                whole(),
                whole(),
                whole(),
            ],
            out_specs=tuple(whole() for _ in range(7)),
            scratch_shapes=[
                pltpu.VMEM((FC * FRAME, features), BF16),
                pltpu.VMEM((nz, rows, HD), F32),
                pltpu.VMEM((nz, rows, HD), F32),
                pltpu.VMEM((rows, HD), F32),
                pltpu.VMEM((nx, rows, HD), F32),
                pltpu.VMEM((2 * ny, 9, 16, BLOCK), BF16),
                dma(()),
                dma((nz,)),
                dma((nz,)),
                dma((nx,)),
                dma((nx,)),
                dma((ny,)),
                dma((ny,)),
                dma((nz,)),
                dma((nz,)),
                dma((nz,)),
                dma((nz,)),
                dma((ny,)),
                dma((ny,)),
                dma((ny,)),
                dma((ny,)),
            ],
            compiler_params=pltpu.CompilerParams(
                collective_id=0, has_side_effects=True, vmem_limit_bytes=40 * 1024 * 1024
            ),
            name="encode_and_move",
        )(
            clip_shape.reshape(3),
            packing.reshape(4),
            clip_features.reshape(FC * FRAME, features),
            conv_weight.reshape(-1, features),
            embed_weight,
            mod_scale.reshape(1, -1),
            mod_shift.reshape(1, -1),
            qkv_weight,
        )
        out = pl.pallas_call(
            functools.partial(attend_kernel, ny, nz),
            out_shape=jax.ShapeDtypeStruct((BLOCK, 2 * ny * HD), BF16),
            in_specs=[whole() for _ in range(9)],
            out_specs=whole(),
            compiler_params=pltpu.CompilerParams(vmem_limit_bytes=40 * 1024 * 1024),
            name="attend",
        )(*moved, q_gain.reshape(1, -1), k_gain.reshape(1, -1))
        return out[None]

    return jax.shard_map(
        on_device,
        mesh=mesh,
        in_specs=(
            P("enc", "seq", None, None, None, None),
            P("enc", "seq", None),
            P("enc", "seq", None, None),
            P(),
            P(),
            P(),
            P(),
            P(None, "seq", "enc"),
            P(),
            P(),
        ),
        out_specs=P("seq", "enc", None),
        check_vma=False,
    )
```

time: 266 us -> 54 us (0.20)
  blocking collectives: 87.3 us -> 0 us
  matrix products: 58 us -> 0 us
  Pallas kernels: 0 us -> 46.9 us
  waiting for transfers between devices: 40.5 us -> 0 us
  other arithmetic: 38.9 us -> 0 us
  between operations: 20.2 us -> 0.03 us
  local copies, waits for them, and re-layouts: 19.3 us -> 6.69 us
    dot_general x49 -> x0, matrix products: 58 us -> none  [the longest x27 15.9 us: encode(): lax.dot_general(conv_weight[9 * tap_depth + 3 * tap_row + tap_col], shift...]
    all_gather x3 -> x0, blocking collectives: 54.8 us -> none  [the longest x1 20.9 us: on_device(): part_plan = lax.all_gather(plan_rows, 'enc', axis=0, tiled=True)]
    pallas_call x0 -> x2, Pallas kernels: none -> 46.9 us  [the longest x1 41.1 us: on_device(): pl.pallas_call(functools.partial(move_kernel, ny, nz, nx), out_shape=(jax...]
    all_gather x2 -> x0, waiting for transfers between devices: 39.8 us -> none  [the longest x1 39.8 us: on_device(): lax.all_gather((embedded_own, seg_own.reshape(-1)), 'enc', axis=0, tiled=...]
    all_to_all x1 -> x0, blocking collectives: 21.8 us -> none  [on_device(): lax.all_to_all(attended, 'enc', split_axis=0, concat_axis=1, tiled=True)]
    reduce_sum x10 -> x0, other arithmetic: 18.2 us -> none  [the longest x4 9.11 us: norm_project(): row_var = jnp.mean(centered * centered, -1, keepdims=True)]
    slice x3 -> x0, local copies, waits for them, and re-layouts: 11.5 us -> none  [the longest x2 10.1 us: encode(): padded[tap_depth:tap_depth + frames_cap, tap_row:tap_row + height_cap, ta...]
    unnamed x1 -> x0, blocking collectives: 10.6 us -> none
  transfers between devices with their start and end apart: 2 -> 0, of which waited for: 1 -> 0; matrix products, arithmetic and copies ran while one was open for 16% -> 0% of each run, Pallas kernels for 0% -> 0%
where the time goes in v1:
time: 54 us; the launch traced here: 53.6 us
  Pallas kernels  46.9 us (87%)
  local copies, waits for them, and re-layouts  6.69 us (12%)
    pallas_call x1, Pallas kernels, on_device(): pl.pallas_call(functools.partial(move_kernel, ny, nz, nx), out_shape=(jax...  41.1 us
    unnamed x20, local copies, waits for them, and re-layouts  6.6 us
    pallas_call x1, Pallas kernels, on_device(): pl.pallas_call(functools.partial(attend_kernel, ny, nz), out_shape=jax.Sh...  5.83 us

profile of v1, /device:TPU:1, one launch (start us, length us, event | category | flops | bytes accessed | tf_op | source)
XLA Modules:
  0.0 53.6 jit_solution(14765485949029307411)
XLA Ops:
  0.0 0.0 copy-start.4
  0.0 0.0 copy-start.9
  0.0 0.7 %copy-done.9 = s32[1,1,2,2]{3,2,1,0:T(2,128)S(1)} copy-done((s32[1,1,2,2]{3,2,1,0:T(2,128)S(1)}, s32[1,1,2,2]{3,2,1,0:T(2,128)}, u32[]{:S(2)}) %copy-start.9) | copy-done | bytes 40
  0.7 0.0 copy-start.6
  0.7 0.1 reshape.25.plan_ref
  0.8 0.0 copy-done.4
  0.8 0.6 %copy-done.6 = s32[1,1,3]{2,1,0:T(1,128)S(1)} copy-done((s32[1,1,3]{2,1,0:T(1,128)S(1)}, s32[1,1,3]{2,1,0:T(1,128)}, u32[]{:S(2)}) %copy-start.6) | copy-done | bytes 36
  1.4 0.0 copy-start
  1.4 1.2 %copy-done = bf16[1,1,4,16,16,512]{5,4,3,2,1,0:T(8,128)(2,1)S(1)} copy-done((bf16[1,1,4,16,16,512]{5,4,3,2,1,0:T(8,128)(2,1)S(1)}, bf16[1,1,4,16,16,512]{5,4,3,2,1,0:T(8,128)(2,1)}, u32[]{:S(2)}) %copy-start) | copy-done | bytes 1048600
  2.6 0.0 copy-start.1
  2.6 1.0 %copy-done.1 = bf16[27,16,512]{2,1,0:T(8,128)(2,1)S(1)} copy-done((bf16[27,16,512]{2,1,0:T(8,128)(2,1)S(1)}, bf16[27,16,512]{2,1,0:T(8,128)(2,1)}, u32[]{:S(2)}) %copy-start.1) | copy-done | bytes 442392
  3.6 0.0 copy-start.2
  3.6 0.9 %copy-done.2 = bf16[64,2048]{1,0:T(8,128)(2,1)S(1)} copy-done((bf16[64,2048]{1,0:T(8,128)(2,1)S(1)}, bf16[64,2048]{1,0:T(8,128)(2,1)}, u32[]{:S(2)}) %copy-start.2) | copy-done | bytes 262168
  4.5 0.0 copy-start.3
  4.5 0.8 %copy-done.3 = bf16[3,64,128]{2,1,0:T(8,128)(2,1)S(1)} copy-done((bf16[3,64,128]{2,1,0:T(8,128)(2,1)S(1)}, bf16[3,64,128]{2,1,0:T(8,128)(2,1)}, u32[]{:S(2)}) %copy-start.3) | copy-done | bytes 49176
  5.3 0.0 copy-start.5
  5.3 0.7 %copy-done.5 = f32[2048]{0:T(1024)S(1)} copy-done((f32[2048]{0:T(1024)S(1)}, f32[2048]{0:T(1024)}, u32[]{:S(2)}) %copy-start.5) | copy-done | bytes 8216
  6.0 41.1 %encode_and_move.1 = (bf16[256,64]{1,0:T(8,128)(2,1)S(1)}, bf16[128,64]{1,0:T(8,128)(2,1)S(1)}, f32[256,128]{1,0:T(8,128)S(1)}, f32[128,128]{1,0:T(8,128)S(1)}, ...) custom-call(s32[3]{0:T(128)S(1)} %bitcast.12, ...), custom_call_target="tpu_custom_call" | custom-call | tf_op jit(solution)/shard_map/encode_and_move/pallas_call | solution.py:406
  47.1 0.0 copy-start.7
  47.1 0.0 copy-start.8
  47.1 0.6 %copy-done.7 = f32[128]{0:T(128)S(1)} copy-done((f32[128]{0:T(128)S(1)}, f32[128]{0:T(128)}, u32[]{:S(2)}) %copy-start.7) | copy-done | bytes 536
  47.8 0.0 copy-done.8
  47.8 5.8 %attend.1 = bf16[128,2048]{1,0:T(8,128)(2,1)} custom-call(bf16[256,64]{1,0:T(8,128)(2,1)S(1)} %get-tuple-element.12.xt_ref, bf16[128,64]{1,0:T(8,128)(2,1)S(1)} %get-tuple-element.13.xq_ref, f32[256,128]{1,0:T(8,128)S(1)} %get-tuple-element.14.rk_ref, f32[128,128]{1,0:T(8,128)S(1)} %get-tuple-element.15.rq_ref, f32[128,256]{1,0:T(8,128)S(1)} %get-tuple-element.16.same_ref, ...), custom_call_target="tpu_custom_call" | custom-call | tf_op jit(solution)/shard_map/attend/pallas_call | solution.py:465
Async XLA Ops:
  0.0 0.8 %copy-start.4 = (f32[2048]{0:T(1024)S(1)}, f32[2048]{0:T(1024)}, u32[]{:S(2)}) copy-start(f32[2048]{0:T(1024)} %param.16) | copy-start | bytes 24580
  0.0 0.7 %copy-start.9 = (s32[1,1,2,2]{3,2,1,0:T(2,128)S(1)}, s32[1,1,2,2]{3,2,1,0:T(2,128)}, u32[]{:S(2)}) copy-start(s32[1,1,2,2]{3,2,1,0:T(2,128)} %param.12) | copy-start | bytes 52
  0.7 0.7 %copy-start.6 = (s32[1,1,3]{2,1,0:T(1,128)S(1)}, s32[1,1,3]{2,1,0:T(1,128)}, u32[]{:S(2)}) copy-start(s32[1,1,3]{2,1,0:T(1,128)} %param.11) | copy-start | bytes 40
  1.4 1.2 %copy-start = (bf16[1,1,4,16,16,512]{5,4,3,2,1,0:T(8,128)(2,1)S(1)}, bf16[1,1,4,16,16,512]{5,4,3,2,1,0:T(8,128)(2,1)}, u32[]{:S(2)}) copy-start(bf16[1,1,4,16,16,512]{5,4,3,2,1,0:T(8,128)(2,1)} %param.10) | copy-start | bytes 3145732
  2.6 1.0 %copy-start.1 = (bf16[27,16,512]{2,1,0:T(8,128)(2,1)S(1)}, bf16[27,16,512]{2,1,0:T(8,128)(2,1)}, u32[]{:S(2)}) copy-start(bf16[27,16,512]{2,1,0:T(8,128)(2,1)} %param.13) | copy-start | bytes 1327108
  3.6 0.9 %copy-start.2 = (bf16[64,2048]{1,0:T(8,128)(2,1)S(1)}, bf16[64,2048]{1,0:T(8,128)(2,1)}, u32[]{:S(2)}) copy-start(bf16[64,2048]{1,0:T(8,128)(2,1)} %embed_ref.1) | copy-start | bytes 786436
  4.5 0.8 %copy-start.3 = (bf16[3,64,128]{2,1,0:T(8,128)(2,1)S(1)}, bf16[3,64,128]{2,1,0:T(8,128)(2,1)}, u32[]{:S(2)}) copy-start(bf16[3,64,128]{2,1,0:T(8,128)(2,1)} %w_ref.1) | copy-start | bytes 147460
  5.3 0.7 %copy-start.5 = (f32[2048]{0:T(1024)S(1)}, f32[2048]{0:T(1024)}, u32[]{:S(2)}) copy-start(f32[2048]{0:T(1024)} %param.15) | copy-start | bytes 24580
  47.1 0.7 %copy-start.7 = (f32[128]{0:T(128)S(1)}, f32[128]{0:T(128)}, u32[]{:S(2)}) copy-start(f32[128]{0:T(128)} %param.18) | copy-start | bytes 1540
  47.1 0.7 %copy-start.8 = (f32[128]{0:T(128)S(1)}, f32[128]{0:T(128)}, u32[]{:S(2)}) copy-start(f32[128]{0:T(128)} %param.19) | copy-start | bytes 1540

commit v2 on v1

v2 whole, which is shorter than its diff:
```python
import functools
import math

import jax
import jax.numpy as jnp
from jax import lax
from jax.experimental import pallas as pl
from jax.experimental.pallas import tpu as pltpu
from jax.sharding import PartitionSpec as P

MESH = pl.DeviceIdType.MESH
F32 = jnp.float32
BF16 = jnp.bfloat16
EPS = 1e-06
LATF = 64
LAT = 16
TOK = 256
BLOCK = 128
FRAME = 256
FC = 4
HD = 128


def mod(a, n):
    return lax.rem(a, n)


def near_first(n):
    order = []
    for d in range(1, n // 2 + 1):
        order.append(d)
        if n - d != d:
            order.append(n - d)
    return order


def split_bf16(value, terms):
    parts = []
    for _ in range(terms):
        part = value.astype(BF16)
        parts.append(part)
        value = value - part.astype(F32)
    return parts


def nt_dot(a, b):
    return lax.dot_general(a, b, (((1,), (1,)), ((), ())), preferred_element_type=F32)


def partial_fold(s, embed_ref, scale_ref, shift_ref, w_ref):
    embed = embed_ref[...].astype(F32)
    mean = jnp.mean(embed, -1, keepdims=True)
    window = pl.ds(pl.multiple_of((s // 2) * 128, 128), 128)
    a_part = (embed_ref[:, window].astype(F32) - mean) * (1.0 + scale_ref[:, window])
    shift_rows = jnp.broadcast_to(shift_ref[:, window], (16, 128))
    lhs = jnp.concatenate([a_part, shift_rows], 0)
    hi, lo = split_bf16(lhs, 2)
    lhs2 = jnp.concatenate([hi, lo], 1)
    half = lax.broadcasted_iota(jnp.int32, (128, 3 * HD), 0) // 64
    w_all = jnp.concatenate([w_ref[0], w_ref[1], w_ref[2]], 1).astype(F32)
    w_two = jnp.concatenate([w_all, w_all], 0)
    w_pad = jnp.where(half == mod(s, 2), w_two, 0.0).astype(BF16)
    rhs = jnp.concatenate([w_pad, w_pad], 0)
    return jnp.dot(lhs2, rhs, preferred_element_type=F32)


def token_places(frames, height, width):
    slot = lax.broadcasted_iota(jnp.int32, (1, TOK), 1).astype(F32)
    zero = jnp.zeros((1, TOK), jnp.int32)
    frames_v = (zero + frames).astype(F32)
    half_h = (zero + height).astype(F32) * 0.5
    half_w = (zero + width).astype(F32) * 0.5
    per_frame = half_h * half_w
    t = jnp.floor((slot + 0.5) / per_frame)
    within = slot - t * per_frame
    r = jnp.floor((within + 0.5) / half_w)
    q = within - r * half_w
    count = frames_v * per_frame
    return jnp.where(slot < count, t * FRAME + r * 32.0 + q * 2.0, -1.0), count


def clip_tokens(frames, height, width, feat_ref, conv_ref):
    lane = lax.broadcasted_iota(jnp.int32, (1, FRAME), 1)
    row, col = lane // 16, lane % 16
    inside = (row < height) & (col < width)
    conv = conv_ref[...]
    places, count = token_places(frames, height, width)
    spot = lax.broadcasted_iota(jnp.int32, (FRAME, TOK), 0).astype(F32)
    products = []
    tokens = jnp.zeros((LATF, TOK), F32)
    taps = 9 * LAT
    for t in range(FC):
        here = nt_dot(conv, feat_ref[t * FRAME : (t + 1) * FRAME, :])
        keep = inside & (lane < jnp.where(t < frames, FRAME, 0))
        products.append(jnp.where(keep, here, 0.0))
        summed = products[t][2 * taps :]
        if t >= 1:
            summed = summed + products[t - 1][taps : 2 * taps]
        if t >= 2:
            summed = summed + products[t - 2][:taps]
        third = 3 * LAT
        rows = summed[third : 2 * third]
        rows = rows + jnp.where(row >= 1, pltpu.roll(summed[:third], 16, 1), 0.0)
        rows = rows + jnp.where(row <= 14, pltpu.roll(summed[2 * third :], FRAME - 16, 1), 0.0)
        latent = rows[LAT : 2 * LAT]
        latent = latent + jnp.where(col >= 1, pltpu.roll(rows[:LAT], 1, 1), 0.0)
        latent = latent + jnp.where(col <= 14, pltpu.roll(rows[2 * LAT :], FRAME - 1, 1), 0.0)
        latent = latent.astype(BF16).astype(F32)
        phases = [latent] + [pltpu.roll(latent, FRAME - d, 1) for d in (1, 16, 17)]
        phases = jnp.concatenate(phases, 0).astype(BF16)
        pick = jnp.where(spot + float(t * FRAME) == places, 1.0, 0.0).astype(BF16)
        tokens = tokens + jnp.dot(phases, pick, preferred_element_type=F32)
    out_row = lax.broadcasted_iota(jnp.int32, (LATF, LATF), 0)
    in_row = lax.broadcasted_iota(jnp.int32, (LATF, LATF), 1)
    swap = jnp.where(in_row == (out_row % 4) * LAT + out_row // 4, 1.0, 0.0).astype(BF16)
    tokens = jnp.dot(swap, tokens.astype(BF16), preferred_element_type=F32)
    return tokens.astype(BF16), count


def gram_terms(embed_ref):
    embed = embed_ref[...]
    features = embed.shape[1]
    both = nt_dot(embed, embed)
    wide = embed.astype(F32)
    mean_col = jnp.mean(wide, -1, keepdims=True)
    ones = jnp.ones((8, features), BF16)
    mean_row = nt_dot(ones, embed)[:1] * (1.0 / features)
    gram = both * (1.0 / features) - mean_col * mean_row
    return jnp.concatenate(split_bf16(gram, 3), 0)


def resplit(tile):
    row = lax.broadcasted_iota(jnp.int32, tile.shape, 0)
    total = tile + pltpu.roll(tile, tile.shape[0] - 3, 0)
    high = total.astype(BF16).astype(F32)
    low = pltpu.roll(total - high, 3, 0)
    return jnp.where(row < 3, high, jnp.where(row < 6, low, 0.0))


def pick_clip(e, count, x_all, gram):
    chosen = jnp.zeros((2, 4, 16, BLOCK), F32)
    is1 = jnp.zeros((1, BLOCK), F32)
    live = jnp.zeros((1, BLOCK), F32)
    me = (jnp.zeros((1, BLOCK), jnp.int32) + e).astype(F32)
    for j in range(count):
        info = x_all[j, 8].astype(F32)
        here1 = jnp.where(info[1:2] == me, 1.0, 0.0)
        here = jnp.where(info[0:1] == me, 1.0, 0.0) + here1
        is1 = is1 + here1
        live = live + here * info[2:3]
        chosen = chosen + x_all[j, 0:8].astype(F32).reshape(2, 4, 16, BLOCK) * here
    chosen = chosen.reshape(2, LATF, BLOCK)
    xt = jnp.concatenate([chosen[0].T, chosen[1].T], 0)
    xt16 = xt.astype(BF16)
    mixed = jnp.dot(jnp.concatenate([xt16, xt16, xt16], 1), gram, preferred_element_type=F32)
    var = jnp.sum(mixed * xt, -1, keepdims=True)
    scaled = xt * lax.rsqrt(jnp.maximum(var, 0.0) + EPS)
    high, low = split_bf16(scaled, 2)
    keys = jnp.concatenate([high, low], 1)
    rows = jnp.where(is1 > 0.5, keys[BLOCK:].astype(F32), keys[:BLOCK].astype(F32)).astype(BF16)
    keys = jnp.concatenate([keys, jnp.ones((TOK, 16), BF16)], 1)
    rows = jnp.concatenate([rows, jnp.ones((BLOCK, 16), BF16)], 1)
    q_slot = lax.broadcasted_iota(jnp.int32, (BLOCK, BLOCK), 0).astype(F32) + is1 * BLOCK
    q_live = jnp.where(q_slot < live, 1.0, 0.0)
    same = []
    for b in range(2):
        k_slot = lax.broadcasted_iota(jnp.int32, (1, BLOCK), 1).astype(F32) + float(b * BLOCK)
        k_live = jnp.where(k_slot < live, 1.0, 0.0)
        same.append(jnp.where(q_live == k_live, 1.0, 0.0))
    return keys, rows, jnp.concatenate(same, 1)


def attend_head(keys, rows, same, fold, tail, gain):
    row = lax.broadcasted_iota(jnp.int32, (16, HD), 0)
    tail = tail.astype(F32)
    bias = [jnp.where((row == j) | (row == j + 3), tail, 0.0).astype(BF16) for j in range(3)]
    q = jnp.dot(rows, jnp.concatenate([fold[0], fold[0], bias[0]], 0), preferred_element_type=F32)
    kv_fold = jnp.concatenate(fold[1:], 1)
    kv_bias = jnp.concatenate(bias[1:], 1)
    kv = jnp.dot(
        keys, jnp.concatenate([kv_fold, kv_fold, kv_bias], 0), preferred_element_type=F32
    )
    k = kv[:, :HD]
    v = kv[:, HD:].astype(BF16)
    q = q * (lax.rsqrt(jnp.mean(q * q, -1, keepdims=True) + EPS)) * gain
    k = k * lax.rsqrt(jnp.mean(k * k, -1, keepdims=True) + EPS)
    scores = nt_dot(q.astype(BF16), k.astype(BF16))
    weights = (jnp.exp2(scores) * same).astype(BF16)
    ones = jnp.ones((TOK, HD), BF16)
    mixed = jnp.dot(weights, jnp.concatenate([v, ones], 1), preferred_element_type=F32)
    return (mixed[:, :HD] / mixed[:, HD:]).astype(BF16)


def whole_kernel(
    ny,
    nz,
    nx,
    dims_ref,
    plan_ref,
    feat_hbm,
    conv_hbm,
    embed_hbm,
    scale_hbm,
    shift_hbm,
    w_hbm,
    qg_hbm,
    kg_hbm,
    out_ref,
    feat_ref,
    conv_ref,
    embed_ref,
    scale_ref,
    shift_ref,
    w_ref,
    qg_ref,
    kg_ref,
    stage,
    x_in,
    z_own,
    z_in,
    folds,
    x_all,
    in_sem,
    sendx,
    recvx,
    sendz,
    recvz,
    sendy,
    recvy,
    sendq,
    recvq,
    sendc,
    recvc,
    sendt,
    recvt,
    sendu,
    recvu,
):
    e = lax.axis_index("enc")
    s = lax.axis_index("seq")
    y, c = e // 2, mod(e, 2)
    z, x = s // nx, mod(s, nx)
    part_rows = LATF // nx
    fold_rows = 3 * part_rows

    def at_y(d):
        return {"enc": mod(y + d, ny) * 2 + c, "seq": s}

    def at_z(d):
        return {"enc": e, "seq": mod(z + d, nz) * nx + x}

    def at_x(d):
        return {"enc": e, "seq": z * nx + mod(x + d, nx)}

    sibling = {"enc": y * 2 + 1 - c, "seq": s}

    barrier = pltpu.get_barrier_semaphore()
    peers = [at_z(d) for d in reversed(near_first(nz))] + [at_y(d) for d in reversed(near_first(ny))]
    peers += [at_x(d) for d in reversed(near_first(nx))] + [sibling]
    for peer in peers:
        pl.semaphore_signal(barrier, inc=1, device_id=peer, device_id_type=MESH)

    loads = {}
    for i, (name, src, dst) in enumerate(
        [
            ("embed", embed_hbm, embed_ref),
            ("w", w_hbm, w_ref),
            ("scale", scale_hbm, scale_ref),
            ("shift", shift_hbm, shift_ref),
            ("conv", conv_hbm, conv_ref),
            ("feat", feat_hbm, feat_ref),
            ("qg", qg_hbm, qg_ref),
            ("kg", kg_hbm, kg_ref),
        ]
    ):
        loads[name] = pltpu.make_async_copy(src, dst, in_sem.at[i])
        loads[name].start()

    sends = []

    def send(src, dst, send_sem, recv_sem, peer):
        copy = pltpu.make_async_remote_copy(
            src_ref=src,
            dst_ref=dst,
            send_sem=send_sem,
            recv_sem=recv_sem,
            device_id=peer,
            device_id_type=MESH,
        )
        copy.start()
        sends.append(copy)
        return copy

    for name in ("embed", "w", "scale", "shift"):
        loads[name].wait()
    part = partial_fold(s, embed_ref, scale_ref, shift_ref, w_ref)
    row16 = lax.broadcasted_iota(jnp.int32, (16, HD), 0)
    bias = jnp.zeros((16, HD), F32)
    for j in range(3):
        bias = jnp.where(row16 == j, part[LATF : LATF + 16, j * HD : (j + 1) * HD], bias)
    bias = resplit(bias).astype(BF16)
    for g in range(nx):
        for j in range(3):
            stage[g, j * part_rows : (j + 1) * part_rows, :] = part[
                g * part_rows : (g + 1) * part_rows, j * HD : (j + 1) * HD
            ].astype(BF16)
        stage[g, fold_rows:, :] = bias

    pl.semaphore_wait(barrier, len(peers))

    over_x = [
        send(stage.at[mod(x + d, nx)], x_in.at[d], sendx.at[d], recvx.at[d], at_x(d))
        for d in near_first(nx)
    ]

    for name in ("conv", "feat"):
        loads[name].wait()
    frames, height, width = dims_ref[0, 0, 0], dims_ref[0, 0, 1], dims_ref[0, 0, 2]
    tokens, count = clip_tokens(frames, height, width, feat_ref, conv_ref)
    for b in range(2):
        for i in range(4):
            x_all[e, 4 * b + i] = tokens[16 * i : 16 * i + 16, b * BLOCK : (b + 1) * BLOCK]
    owner0 = (jnp.zeros((16, BLOCK), jnp.int32) + plan_ref[0, 0, 0, 0]).astype(F32)
    owner1 = (jnp.zeros((16, BLOCK), jnp.int32) + plan_ref[0, 0, 1, 0]).astype(F32)
    meta = jnp.where(row16 == 0, owner0, jnp.where(row16 == 1, owner1, count[:, :BLOCK]))
    x_all[e, 8] = meta.astype(BF16)
    x_first = [
        send(x_all.at[e], x_all.at[e], sendt.at[d], recvt.at[d], at_y(d)) for d in near_first(ny)
    ]
    x_second = [send(x_all.at[e], x_all.at[e], sendu.at[0], recvu.at[0], sibling)]

    def finish(total):
        return jnp.concatenate([total[:fold_rows], resplit(total[fold_rows:])], 0).astype(BF16)

    total = stage[x].astype(F32)
    for copy in over_x:
        copy.wait_recv()
    for d in range(1, nx):
        total = total + x_in[d].astype(F32)
    z_own[...] = finish(total)
    over_z = [
        send(z_own, z_in.at[d], sendz.at[d], recvz.at[d], at_z(d))
        for d in reversed(near_first(nz))
    ]
    gram = gram_terms(embed_ref)

    def pass_tokens(d, copy):
        copy.wait_recv()
        source = mod(y - d + ny, ny) * 2 + c
        x_second.append(
            send(x_all.at[source], x_all.at[source], sendu.at[d], recvu.at[d], sibling)
        )

    arriving = list(zip(near_first(ny), x_first))
    early = len(arriving) // 2
    for d, copy in arriving[:early]:
        pass_tokens(d, copy)
    total = z_own[...].astype(F32)
    for copy in over_z:
        copy.wait_recv()
    for d in range(1, nz):
        total = total + z_in[d].astype(F32)
    folds[c, y, x] = finish(total)

    over_y = {}
    for d in near_first(ny):
        mine = folds.at[c, y, x]
        over_y[d] = send(mine, mine, sendy.at[d], recvy.at[d], at_y(d))
    quarters = {}
    crossed = {}

    def source_y(d):
        return mod(y - d + ny, ny)

    def spread(d):
        if d:
            over_y[d].wait_recv()
        piece = folds.at[c, source_y(d), x, pl.ds(0, fold_rows)]
        quarters[d] = [
            send(piece, piece, sendq.at[d, dx], recvq.at[d, dx], at_x(dx))
            for dx in near_first(nx)
        ]

    def cross(d):
        for copy in quarters[d]:
            copy.wait_recv()
        piece = folds.at[c, source_y(d)]
        crossed[d] = send(piece, piece, sendc.at[d], recvc.at[d], sibling)

    spread(0)
    for d, copy in arriving[early:]:
        pass_tokens(d, copy)
    for copy in x_second:
        copy.wait_recv()
    keys, rows, same = pick_clip(e, 2 * ny, x_all, gram)
    for name in ("qg", "kg"):
        loads[name].wait()
    gain = qg_ref[...] * kg_ref[...] * (HD**-0.5 * math.log2(math.e))

    def attend(d, core):
        source = source_y(d)
        fold = [
            folds[core, source, :, j * part_rows : (j + 1) * part_rows, :].reshape(LATF, HD)
            for j in range(3)
        ]
        tail = folds[core, source, x, fold_rows:, :]
        column = pl.ds(pl.multiple_of((2 * source + core) * HD, HD), HD)
        out_ref[:, column] = attend_head(keys, rows, same, fold, tail, gain)

    order = [0] + near_first(ny)
    ahead = 3
    for i in range(1, min(ahead, ny)):
        spread(order[i])
    for i in range(ny):
        if i + ahead < ny:
            spread(order[i + ahead])
        elif i + ahead == ny:
            pass
        cross(order[i]) if order[i] in quarters else None
        attend(order[i], c)
        if i >= 1:
            crossed[order[i - 1]].wait_recv()
            attend(order[i - 1], 1 - c)
    crossed[order[ny - 1]].wait_recv()
    attend(order[ny - 1], 1 - c)
    for copy in sends:
        copy.wait_send()


def whole(memory=pltpu.VMEM):
    return pl.BlockSpec(memory_space=memory)


def solution(mesh):
    ny = mesh.shape["enc"] // 2
    nx = 4 if mesh.shape["seq"] == 32 else 2
    nz = mesh.shape["seq"] // nx
    fold_rows = 3 * LATF // nx
    rows = fold_rows + 16
    dma = pltpu.SemaphoreType.DMA

    def on_device(
        clip_features,
        clip_shape,
        packing,
        conv_weight,
        embed_weight,
        mod_shift,
        mod_scale,
        qkv_weight,
        q_gain,
        k_gain,
    ):
        features = clip_features.shape[-1]
        width = embed_weight.shape[1]
        out = pl.pallas_call(
            functools.partial(whole_kernel, ny, nz, nx),
            out_shape=jax.ShapeDtypeStruct((BLOCK, 2 * ny * HD), BF16),
            in_specs=[whole(pltpu.SMEM)] * 2 + [whole(pl.ANY)] * 8,
            out_specs=whole(),
            scratch_shapes=[
                pltpu.VMEM((FC * FRAME, features), BF16),
                pltpu.VMEM((27 * LAT, features), BF16),
                pltpu.VMEM((LATF, width), BF16),
                pltpu.VMEM((1, width), F32),
                pltpu.VMEM((1, width), F32),
                pltpu.VMEM(qkv_weight.shape, BF16),
                pltpu.VMEM((1, HD), F32),
                pltpu.VMEM((1, HD), F32),
                pltpu.VMEM((nx, rows, HD), BF16),
                pltpu.VMEM((nx, rows, HD), BF16),
                pltpu.VMEM((rows, HD), BF16),
                pltpu.VMEM((nz, rows, HD), BF16),
                pltpu.VMEM((2, ny, nx, rows, HD), BF16),
                pltpu.VMEM((2 * ny, 9, 16, BLOCK), BF16),
                dma((8,)),
                dma((nx,)),
                dma((nx,)),
                dma((nz,)),
                dma((nz,)),
                dma((ny,)),
                dma((ny,)),
                dma((ny, nx)),
                dma((ny, nx)),
                dma((ny,)),
                dma((ny,)),
                dma((ny,)),
                dma((ny,)),
                dma((ny,)),
                dma((ny,)),
            ],
            compiler_params=pltpu.CompilerParams(
                collective_id=0, has_side_effects=True, vmem_limit_bytes=60 * 1024 * 1024
            ),
            name="encode_move_attend",
        )(
            clip_shape,
            packing,
            clip_features.reshape(FC * FRAME, features),
            conv_weight.reshape(-1, features),
            embed_weight,
            mod_scale.reshape(1, -1),
            mod_shift.reshape(1, -1),
            qkv_weight,
            q_gain.reshape(1, -1),
            k_gain.reshape(1, -1),
        )
        return out[None]

    return jax.shard_map(
        on_device,
        mesh=mesh,
        in_specs=(
            P("enc", "seq", None, None, None, None),
            P("enc", "seq", None),
            P("enc", "seq", None, None),
            P(),
            P(),
            P(),
            P(),
            P(None, "seq", "enc"),
            P(),
            P(),
        ),
        out_specs=P("seq", "enc", None),
        check_vma=False,
    )
```

time: 54 us -> 45.3 us (0.84)
  local copies, waits for them, and re-layouts: 6.69 us -> 1.88 us
  Pallas kernels: 46.9 us -> 43.2 us
    unnamed x20 -> x1, local copies, waits for them, and re-layouts: 6.6 us -> 1.88 us
    pallas_call x2 -> x1, Pallas kernels: 46.9 us -> 43.2 us  [on_device(): pl.pallas_call(functools.partial(whole_kernel, ny, nz, nx), out_shape=jax...]
where the time goes in v2:
time: 45.3 us; the launch traced here: 45.1 us
  Pallas kernels  43.2 us (95%)
  local copies, waits for them, and re-layouts  1.88 us (4%)
    pallas_call x1, Pallas kernels, on_device(): pl.pallas_call(functools.partial(whole_kernel, ny, nz, nx), out_shape=jax...  43.2 us
    unnamed x1, local copies, waits for them, and re-layouts  1.88 us

profile of v2, /device:TPU:1, one launch (start us, length us, event | category | flops | bytes accessed | tf_op | source)
XLA Modules:
  0.0 45.1 jit_solution(9048585567247088755)
XLA Ops:
  0.0 43.2 %encode_move_attend.1 = bf16[128,2048]{1,0:T(8,128)(2,1)} custom-call(s32[1,1,3]{2,1,0:T(1,128)} %dims_ref.1, s32[1,1,2,2]{3,2,1,0:T(2,128)} %plan_ref.1, bf16[1024,512]{1,0:T(8,128)(2,1)} %bitcast.8, bf16[432,512]{1,0:T(8,128)(2,1)} %bitcast.9, bf16[64,2048]{1,0:T(8,128)(2,1)} %embed_hbm.1, f32[1,2048]{1,0:T(1,128)} %bitcast.10, f32[1,2048]{1,0:T(1,128)} %bitcast.11, ...), custom_call_target="tpu_custom_call" | custom-call | tf_op jit(solution)/shard_map/encode_move_attend/pallas_call | solution.py:456
  43.2 1.9 %copy.12 = bf16[1,128,2048]{2,1,0:T(8,128)(2,1)} copy(bf16[1,128,2048]{2,1,0:T(8,128)(2,1)} %bitcast.7) | data formatting | bytes 1048576

commit v3 on v2

--- a/solution.py
+++ b/solution.py
@@ -79,17 +79,16 @@
     return jnp.where(slot < count, t * FRAME + r * 32.0 + q * 2.0, -1.0), count
 
 
-def clip_tokens(frames, height, width, feat_ref, conv_ref):
+def clip_frames(first, last, state, frames, height, width, feat_ref, conv_ref):
+    products, tokens = state
     lane = lax.broadcasted_iota(jnp.int32, (1, FRAME), 1)
     row, col = lane // 16, lane % 16
     inside = (row < height) & (col < width)
     conv = conv_ref[...]
-    places, count = token_places(frames, height, width)
+    places, _ = token_places(frames, height, width)
     spot = lax.broadcasted_iota(jnp.int32, (FRAME, TOK), 0).astype(F32)
-    products = []
-    tokens = jnp.zeros((LATF, TOK), F32)
     taps = 9 * LAT
-    for t in range(FC):
+    for t in range(first, last):
         here = nt_dot(conv, feat_ref[t * FRAME : (t + 1) * FRAME, :])
         keep = inside & (lane < jnp.where(t < frames, FRAME, 0))
         products.append(jnp.where(keep, here, 0.0))
@@ -110,11 +109,14 @@
         phases = jnp.concatenate(phases, 0).astype(BF16)
         pick = jnp.where(spot + float(t * FRAME) == places, 1.0, 0.0).astype(BF16)
         tokens = tokens + jnp.dot(phases, pick, preferred_element_type=F32)
+    return products, tokens
+
+
+def in_feature_order(tokens):
     out_row = lax.broadcasted_iota(jnp.int32, (LATF, LATF), 0)
     in_row = lax.broadcasted_iota(jnp.int32, (LATF, LATF), 1)
     swap = jnp.where(in_row == (out_row % 4) * LAT + out_row // 4, 1.0, 0.0).astype(BF16)
-    tokens = jnp.dot(swap, tokens.astype(BF16), preferred_element_type=F32)
-    return tokens.astype(BF16), count
+    return jnp.dot(swap, tokens.astype(BF16), preferred_element_type=F32).astype(BF16)
 
 
 def gram_terms(embed_ref):
@@ -158,8 +160,6 @@
     high, low = split_bf16(scaled, 2)
     keys = jnp.concatenate([high, low], 1)
     rows = jnp.where(is1 > 0.5, keys[BLOCK:].astype(F32), keys[:BLOCK].astype(F32)).astype(BF16)
-    keys = jnp.concatenate([keys, jnp.ones((TOK, 16), BF16)], 1)
-    rows = jnp.concatenate([rows, jnp.ones((BLOCK, 16), BF16)], 1)
     q_slot = lax.broadcasted_iota(jnp.int32, (BLOCK, BLOCK), 0).astype(F32) + is1 * BLOCK
     q_live = jnp.where(q_slot < live, 1.0, 0.0)
     same = []
@@ -170,33 +170,32 @@
     return keys, rows, jnp.concatenate(same, 1)
 
 
-def attend_head(keys, rows, same, fold, tail, gain):
-    row = lax.broadcasted_iota(jnp.int32, (16, HD), 0)
+def project_head(keys, rows, fold, tail, gain):
     tail = tail.astype(F32)
-    bias = [jnp.where((row == j) | (row == j + 3), tail, 0.0).astype(BF16) for j in range(3)]
-    q = jnp.dot(rows, jnp.concatenate([fold[0], fold[0], bias[0]], 0), preferred_element_type=F32)
+    bias = tail[0:3] + tail[3:6]
+    q_fold = jnp.concatenate([fold[0], fold[0]], 0)
     kv_fold = jnp.concatenate(fold[1:], 1)
-    kv_bias = jnp.concatenate(bias[1:], 1)
-    kv = jnp.dot(
-        keys, jnp.concatenate([kv_fold, kv_fold, kv_bias], 0), preferred_element_type=F32
-    )
-    k = kv[:, :HD]
-    v = kv[:, HD:].astype(BF16)
-    q = q * (lax.rsqrt(jnp.mean(q * q, -1, keepdims=True) + EPS)) * gain
+    q = jnp.dot(rows, q_fold, preferred_element_type=F32) + bias[0:1]
+    kv = jnp.dot(keys, jnp.concatenate([kv_fold, kv_fold], 0), preferred_element_type=F32)
+    k = kv[:, :HD] + bias[1:2]
+    q = q * lax.rsqrt(jnp.mean(q * q, -1, keepdims=True) + EPS) * gain
     k = k * lax.rsqrt(jnp.mean(k * k, -1, keepdims=True) + EPS)
-    scores = nt_dot(q.astype(BF16), k.astype(BF16))
-    weights = (jnp.exp2(scores) * same).astype(BF16)
+    return q.astype(BF16), k.astype(BF16), kv[:, HD:].astype(BF16), bias[2:3]
+
+
+def mix_head(q, k, v, v_bias, same):
+    weights = (jnp.exp2(nt_dot(q, k)) * same).astype(BF16)
     ones = jnp.ones((TOK, HD), BF16)
     mixed = jnp.dot(weights, jnp.concatenate([v, ones], 1), preferred_element_type=F32)
-    return (mixed[:, :HD] / mixed[:, HD:]).astype(BF16)
+    return (mixed[:, :HD] / mixed[:, HD:] + v_bias).astype(BF16)
 
 
 def whole_kernel(
     ny,
     nz,
     nx,
-    dims_ref,
-    plan_ref,
+    dims_hbm,
+    plan_hbm,
     feat_hbm,
     conv_hbm,
     embed_hbm,
@@ -205,7 +204,9 @@
     w_hbm,
     qg_hbm,
     kg_hbm,
-    out_ref,
+    out_hbm,
+    dims_ref,
+    plan_ref,
     feat_ref,
     conv_ref,
     embed_ref,
@@ -220,6 +221,7 @@
     z_in,
     folds,
     x_all,
+    out_ref,
     in_sem,
     sendx,
     recvx,
@@ -229,8 +231,9 @@
     recvy,
     sendq,
     recvq,
-    sendc,
-    recvc,
+    sendo,
+    recvo,
+    out_sem,
     sendt,
     recvt,
     sendu,
@@ -267,6 +270,8 @@
             ("w", w_hbm, w_ref),
             ("scale", scale_hbm, scale_ref),
             ("shift", shift_hbm, shift_ref),
+            ("dims", dims_hbm, dims_ref),
+            ("plan", plan_hbm, plan_ref),
             ("conv", conv_hbm, conv_ref),
             ("feat", feat_hbm, feat_ref),
             ("qg", qg_hbm, qg_ref),
@@ -306,17 +311,23 @@
             ].astype(BF16)
         stage[g, fold_rows:, :] = bias
 
+    for name in ("dims", "conv", "feat"):
+        loads[name].wait()
+    clip = (dims_ref[0, 0, 0], dims_ref[0, 0, 1], dims_ref[0, 0, 2])
+    state = ([], jnp.zeros((LATF, TOK), F32))
+    state = clip_frames(0, FC // 2, state, *clip, feat_ref, conv_ref)
+
     pl.semaphore_wait(barrier, len(peers))
 
     over_x = [
         send(stage.at[mod(x + d, nx)], x_in.at[d], sendx.at[d], recvx.at[d], at_x(d))
-        for d in near_first(nx)
+        for d in reversed(near_first(nx))
     ]
 
-    for name in ("conv", "feat"):
-        loads[name].wait()
-    frames, height, width = dims_ref[0, 0, 0], dims_ref[0, 0, 1], dims_ref[0, 0, 2]
-    tokens, count = clip_tokens(frames, height, width, feat_ref, conv_ref)
+    state = clip_frames(FC // 2, FC, state, *clip, feat_ref, conv_ref)
+    tokens = in_feature_order(state[1])
+    _, count = token_places(*clip)
+    loads["plan"].wait()
     for b in range(2):
         for i in range(4):
             x_all[e, 4 * b + i] = tokens[16 * i : 16 * i + 16, b * BLOCK : (b + 1) * BLOCK]
@@ -367,7 +378,6 @@
         mine = folds.at[c, y, x]
         over_y[d] = send(mine, mine, sendy.at[d], recvy.at[d], at_y(d))
     quarters = {}
-    crossed = {}
 
     def source_y(d):
         return mod(y - d + ny, ny)
@@ -381,48 +391,70 @@
             for dx in near_first(nx)
         ]
 
-    def cross(d):
+    def arrived(d):
         for copy in quarters[d]:
             copy.wait_recv()
-        piece = folds.at[c, source_y(d)]
-        crossed[d] = send(piece, piece, sendc.at[d], recvc.at[d], sibling)
-
-    spread(0)
+
+    crossed = []
+    order = [0] + near_first(ny)
+    spread(order[0])
     for d, copy in arriving[early:]:
         pass_tokens(d, copy)
+    for d in order[1:]:
+        spread(d)
     for copy in x_second:
         copy.wait_recv()
-    keys, rows, same = pick_clip(e, 2 * ny, x_all, gram)
+    inputs = [pick_clip(owner, 2 * ny, x_all, gram) for owner in (2 * y + 1 - c, e)]
     for name in ("qg", "kg"):
         loads[name].wait()
     gain = qg_ref[...] * kg_ref[...] * (HD**-0.5 * math.log2(math.e))
-
-    def attend(d, core):
-        source = source_y(d)
-        fold = [
-            folds[core, source, :, j * part_rows : (j + 1) * part_rows, :].reshape(LATF, HD)
-            for j in range(3)
+    stores = []
+
+    def project(heads):
+        projected = []
+        for d, own in heads:
+            keys, rows, _ = inputs[own]
+            fold = [
+                folds[c, source_y(d), :, j * part_rows : (j + 1) * part_rows, :].reshape(LATF, HD)
+                for j in range(3)
+            ]
+            tail = folds[c, source_y(d), x, fold_rows:, :]
+            projected.append(project_head(keys, rows, fold, tail, gain))
+        return projected
+
+    def mix(heads, projected):
+        results = [
+            mix_head(*parts, inputs[own][2]) for (d, own), parts in zip(heads, projected)
         ]
-        tail = folds[core, source, x, fold_rows:, :]
-        column = pl.ds(pl.multiple_of((2 * source + core) * HD, HD), HD)
-        out_ref[:, column] = attend_head(keys, rows, same, fold, tail, gain)
-
-    order = [0] + near_first(ny)
-    ahead = 3
-    for i in range(1, min(ahead, ny)):
-        spread(order[i])
-    for i in range(ny):
-        if i + ahead < ny:
-            spread(order[i + ahead])
-        elif i + ahead == ny:
-            pass
-        cross(order[i]) if order[i] in quarters else None
-        attend(order[i], c)
-        if i >= 1:
-            crossed[order[i - 1]].wait_recv()
-            attend(order[i - 1], 1 - c)
-    crossed[order[ny - 1]].wait_recv()
-    attend(order[ny - 1], 1 - c)
+        for (d, own), result in zip(heads, results):
+            out_ref[own, d] = result
+
+    def deliver(heads):
+        for d, own in heads:
+            column = pl.ds(pl.multiple_of((2 * source_y(d) + c) * HD, HD), HD)
+            target = out_hbm.at[:, column]
+            if own:
+                stores.append(pltpu.make_async_copy(out_ref.at[1, d], target, out_sem.at[d]))
+                stores[-1].start()
+            else:
+                crossed.append(send(out_ref.at[0, d], target, sendo.at[d], recvo.at[d], sibling))
+
+    first_half, second_half = order[: ny // 2 + 1], order[ny // 2 + 1 :]
+    first = [(d, own) for own in (0, 1) for d in first_half]
+    second = [(d, own) for own in (0, 1) for d in second_half]
+    for d in first_half:
+        arrived(d)
+    mix(first, project(first))
+    deliver(first)
+    for d in second_half:
+        arrived(d)
+    second_parts = project(second)
+    mix(second, second_parts)
+    deliver(second)
+    for copy in crossed:
+        copy.wait_recv()
+    for copy in stores:
+        copy.wait()
     for copy in sends:
         copy.wait_send()
 
@@ -456,9 +488,11 @@
         out = pl.pallas_call(
             functools.partial(whole_kernel, ny, nz, nx),
             out_shape=jax.ShapeDtypeStruct((BLOCK, 2 * ny * HD), BF16),
-            in_specs=[whole(pltpu.SMEM)] * 2 + [whole(pl.ANY)] * 8,
-            out_specs=whole(),
+            in_specs=[whole(pltpu.HBM)] * 10,
+            out_specs=whole(pltpu.HBM),
             scratch_shapes=[
+                pltpu.SMEM((1, 1, 3), jnp.int32),
+                pltpu.SMEM((1, 1, 2, 2), jnp.int32),
                 pltpu.VMEM((FC * FRAME, features), BF16),
                 pltpu.VMEM((27 * LAT, features), BF16),
                 pltpu.VMEM((LATF, width), BF16),
@@ -473,7 +507,8 @@
                 pltpu.VMEM((nz, rows, HD), BF16),
                 pltpu.VMEM((2, ny, nx, rows, HD), BF16),
                 pltpu.VMEM((2 * ny, 9, 16, BLOCK), BF16),
-                dma((8,)),
+                pltpu.VMEM((2, ny, BLOCK, HD), BF16),
+                dma((10,)),
                 dma((nx,)),
                 dma((nx,)),
                 dma((nz,)),
@@ -482,6 +517,7 @@
                 dma((ny,)),
                 dma((ny, nx)),
                 dma((ny, nx)),
+                dma((ny,)),
                 dma((ny,)),
                 dma((ny,)),
                 dma((ny,)),

time: 45.3 us -> 38.5 us (0.85)
  Pallas kernels: 43.2 us -> 36.4 us
    pallas_call x1, Pallas kernels: 43.2 us -> 36.4 us  [on_device(): pl.pallas_call(functools.partial(whole_kernel, ny, nz, nx), out_shape=jax...]
where the time goes in v3:
time: 38.5 us; the launch traced here: 38.3 us
  Pallas kernels  36.4 us (95%)
  local copies, waits for them, and re-layouts  1.88 us (5%)
    pallas_call x1, Pallas kernels, on_device(): pl.pallas_call(functools.partial(whole_kernel, ny, nz, nx), out_shape=jax...  36.4 us
    unnamed x1, local copies, waits for them, and re-layouts  1.88 us

profile of v3, /device:TPU:1, one launch (start us, length us, event | category | flops | bytes accessed | tf_op | source)
XLA Modules:
  0.0 38.3 jit_solution(2121991246150653616)
XLA Ops:
  0.0 36.4 %encode_move_attend.1 = bf16[128,2048]{1,0:T(8,128)(2,1)} custom-call(s32[1,1,3]{2,1,0:T(1,128)} %dims_hbm.1, s32[1,1,2,2]{3,2,1,0:T(2,128)} %plan_hbm.1, bf16[1024,512]{1,0:T(8,128)(2,1)} %bitcast.8, bf16[432,512]{1,0:T(8,128)(2,1)} %bitcast.9, bf16[64,2048]{1,0:T(8,128)(2,1)} %embed_hbm.1, f32[1,2048]{1,0:T(1,128)} %bitcast.10, f32[1,2048]{1,0:T(1,128)} %bitcast.11, ...), custom_call_target="tpu_custom_call" | custom-call | tf_op jit(solution)/shard_map/encode_move_attend/pallas_call | solution.py:488
  36.4 1.9 %copy.12 = bf16[1,128,2048]{2,1,0:T(8,128)(2,1)} copy(bf16[1,128,2048]{2,1,0:T(8,128)(2,1)} %bitcast.7) | data formatting | bytes 1048576

commit v4 on v3

--- a/solution.py
+++ b/solution.py
@@ -204,7 +204,7 @@
     w_hbm,
     qg_hbm,
     kg_hbm,
-    out_hbm,
+    out_ref,
     dims_ref,
     plan_ref,
     feat_ref,
@@ -221,7 +221,7 @@
     z_in,
     folds,
     x_all,
-    out_ref,
+    crossing,
     in_sem,
     sendx,
     recvx,
@@ -233,7 +233,6 @@
     recvq,
     sendo,
     recvo,
-    out_sem,
     sendt,
     recvt,
     sendu,
@@ -408,7 +407,6 @@
     for name in ("qg", "kg"):
         loads[name].wait()
     gain = qg_ref[...] * kg_ref[...] * (HD**-0.5 * math.log2(math.e))
-    stores = []
 
     def project(heads):
         projected = []
@@ -427,17 +425,13 @@
             mix_head(*parts, inputs[own][2]) for (d, own), parts in zip(heads, projected)
         ]
         for (d, own), result in zip(heads, results):
-            out_ref[own, d] = result
-
-    def deliver(heads):
-        for d, own in heads:
             column = pl.ds(pl.multiple_of((2 * source_y(d) + c) * HD, HD), HD)
-            target = out_hbm.at[:, column]
             if own:
-                stores.append(pltpu.make_async_copy(out_ref.at[1, d], target, out_sem.at[d]))
-                stores[-1].start()
+                out_ref[:, column] = result
             else:
-                crossed.append(send(out_ref.at[0, d], target, sendo.at[d], recvo.at[d], sibling))
+                crossing[d] = result
+                target = out_ref.at[:, column]
+                crossed.append(send(crossing.at[d], target, sendo.at[d], recvo.at[d], sibling))
 
     first_half, second_half = order[: ny // 2 + 1], order[ny // 2 + 1 :]
     first = [(d, own) for own in (0, 1) for d in first_half]
@@ -445,16 +439,12 @@
     for d in first_half:
         arrived(d)
     mix(first, project(first))
-    deliver(first)
     for d in second_half:
         arrived(d)
     second_parts = project(second)
     mix(second, second_parts)
-    deliver(second)
     for copy in crossed:
         copy.wait_recv()
-    for copy in stores:
-        copy.wait()
     for copy in sends:
         copy.wait_send()
 
@@ -487,9 +477,9 @@
         width = embed_weight.shape[1]
         out = pl.pallas_call(
             functools.partial(whole_kernel, ny, nz, nx),
-            out_shape=jax.ShapeDtypeStruct((BLOCK, 2 * ny * HD), BF16),
+            out_shape=pltpu.VMEM((BLOCK, 2 * ny * HD), BF16),
             in_specs=[whole(pltpu.HBM)] * 10,
-            out_specs=whole(pltpu.HBM),
+            out_specs=whole(),
             scratch_shapes=[
                 pltpu.SMEM((1, 1, 3), jnp.int32),
                 pltpu.SMEM((1, 1, 2, 2), jnp.int32),
@@ -507,7 +497,7 @@
                 pltpu.VMEM((nz, rows, HD), BF16),
                 pltpu.VMEM((2, ny, nx, rows, HD), BF16),
                 pltpu.VMEM((2 * ny, 9, 16, BLOCK), BF16),
-                pltpu.VMEM((2, ny, BLOCK, HD), BF16),
+                pltpu.VMEM((ny, BLOCK, HD), BF16),
                 dma((10,)),
                 dma((nx,)),
                 dma((nx,)),
@@ -517,7 +507,6 @@
                 dma((ny,)),
                 dma((ny, nx)),
                 dma((ny, nx)),
-                dma((ny,)),
                 dma((ny,)),
                 dma((ny,)),
                 dma((ny,)),

time: 38.5 us -> 36.9 us (0.958)
  local copies, waits for them, and re-layouts: 1.88 us -> 0.8 us
  Pallas kernels: 36.4 us -> 36 us
    unnamed x1, local copies, waits for them, and re-layouts: 1.88 us -> 0.8 us
    pallas_call x1, Pallas kernels: 36.4 us -> 36 us  [on_device(): pl.pallas_call(functools.partial(whole_kernel, ny, nz, nx), out_shape=plt...]
where the time goes in v4:
time: 36.9 us; the launch traced here: 36.8 us
  Pallas kernels  36 us (98%)
  local copies, waits for them, and re-layouts  0.8 us (2%)
    pallas_call x1, Pallas kernels, on_device(): pl.pallas_call(functools.partial(whole_kernel, ny, nz, nx), out_shape=plt...  36 us
    unnamed x1, local copies, waits for them, and re-layouts  0.8 us

profile of v4, /device:TPU:1, one launch (start us, length us, event | category | flops | bytes accessed | tf_op | source)
XLA Modules:
  0.0 36.8 jit_solution(7078482811593829441)
XLA Ops:
  0.0 36.0 %encode_move_attend.1 = bf16[128,2048]{1,0:T(8,128)(2,1)S(1)} custom-call(s32[1,1,3]{2,1,0:T(1,128)} %dims_hbm.1, s32[1,1,2,2]{3,2,1,0:T(2,128)} %plan_hbm.1, bf16[1024,512]{1,0:T(8,128)(2,1)} %bitcast.8, bf16[432,512]{1,0:T(8,128)(2,1)} %bitcast.9, bf16[64,2048]{1,0:T(8,128)(2,1)} %embed_hbm.1, f32[1,2048]{1,0:T(1,128)} %bitcast.10, f32[1,2048]{1,0:T(1,128)} %bitcast.11, ...), custom_call_target="tpu_custom_call" | custom-call | tf_op jit(solution)/shard_map/encode_move_attend/pallas_call | solution.py:478
  36.0 0.8 %copy.12 = bf16[1,128,2048]{2,1,0:T(8,128)(2,1)} copy(bf16[1,128,2048]{2,1,0:T(8,128)(2,1)S(1)} %bitcast.7) | data formatting | bytes 1048576

commit v5 on v4

--- a/solution.py
+++ b/solution.py
@@ -280,7 +280,9 @@
         loads[name] = pltpu.make_async_copy(src, dst, in_sem.at[i])
         loads[name].start()
 
-    sends = []
+    def settle(copies):
+        for copy in copies:
+            copy.wait_send()
 
     def send(src, dst, send_sem, recv_sem, peer):
         copy = pltpu.make_async_remote_copy(
@@ -292,7 +294,6 @@
             device_id_type=MESH,
         )
         copy.start()
-        sends.append(copy)
         return copy
 
     for name in ("embed", "w", "scale", "shift"):
@@ -373,7 +374,7 @@
     folds[c, y, x] = finish(total)
 
     over_y = {}
-    for d in near_first(ny):
+    for d in ([1, 7, 2, 6, 4, 3, 5] if ny == 8 else near_first(ny)):
         mine = folds.at[c, y, x]
         over_y[d] = send(mine, mine, sendy.at[d], recvy.at[d], at_y(d))
     quarters = {}
@@ -401,8 +402,10 @@
         pass_tokens(d, copy)
     for d in order[1:]:
         spread(d)
+    settle(over_x + over_z + list(over_y.values()) + x_first)
     for copy in x_second:
         copy.wait_recv()
+    settle(x_second)
     inputs = [pick_clip(owner, 2 * ny, x_all, gram) for owner in (2 * y + 1 - c, e)]
     for name in ("qg", "kg"):
         loads[name].wait()
@@ -442,11 +445,14 @@
     for d in second_half:
         arrived(d)
     second_parts = project(second)
-    mix(second, second_parts)
+    count = len(second_half)
+    mix(second[:count], second_parts[:count])
+    for d in order:
+        settle(quarters[d])
+    mix(second[count:], second_parts[count:])
     for copy in crossed:
         copy.wait_recv()
-    for copy in sends:
-        copy.wait_send()
+    settle(crossed)
 
 
 def whole(memory=pltpu.VMEM):

time: 36.9 us -> 36.6 us (level)
  no operation moved by 1% of the time
where the time goes in v5:
time: 36.6 us; the launch traced here: 36.5 us
  Pallas kernels  35.7 us (98%)
  local copies, waits for them, and re-layouts  0.8 us (2%)
    pallas_call x1, Pallas kernels, on_device(): pl.pallas_call(functools.partial(whole_kernel, ny, nz, nx), out_shape=plt...  35.7 us
    unnamed x1, local copies, waits for them, and re-layouts  0.8 us

profile of v5, /device:TPU:1, one launch (start us, length us, event | category | flops | bytes accessed | tf_op | source)
XLA Modules:
  0.0 36.5 jit_solution(17629189004851360743)
XLA Ops:
  0.0 35.7 %encode_move_attend.1 = bf16[128,2048]{1,0:T(8,128)(2,1)S(1)} custom-call(s32[1,1,3]{2,1,0:T(1,128)} %dims_hbm.1, s32[1,1,2,2]{3,2,1,0:T(2,128)} %plan_hbm.1, bf16[1024,512]{1,0:T(8,128)(2,1)} %bitcast.8, bf16[432,512]{1,0:T(8,128)(2,1)} %bitcast.9, bf16[64,2048]{1,0:T(8,128)(2,1)} %embed_hbm.1, f32[1,2048]{1,0:T(1,128)} %bitcast.10, f32[1,2048]{1,0:T(1,128)} %bitcast.11, ...), custom_call_target="tpu_custom_call" | custom-call | tf_op jit(solution)/shard_map/encode_move_attend/pallas_call | solution.py:484
  35.7 0.8 %copy.12 = bf16[1,128,2048]{2,1,0:T(8,128)(2,1)} copy(bf16[1,128,2048]{2,1,0:T(8,128)(2,1)S(1)} %bitcast.7) | data formatting | bytes 1048576

commit v6 on v5

--- a/solution.py
+++ b/solution.py
@@ -178,8 +178,8 @@
     q = jnp.dot(rows, q_fold, preferred_element_type=F32) + bias[0:1]
     kv = jnp.dot(keys, jnp.concatenate([kv_fold, kv_fold], 0), preferred_element_type=F32)
     k = kv[:, :HD] + bias[1:2]
-    q = q * lax.rsqrt(jnp.mean(q * q, -1, keepdims=True) + EPS) * gain
-    k = k * lax.rsqrt(jnp.mean(k * k, -1, keepdims=True) + EPS)
+    q = q * lax.rsqrt(jnp.sum(q * q, -1, keepdims=True) + HD * EPS) * gain
+    k = k * lax.rsqrt(jnp.sum(k * k, -1, keepdims=True) + HD * EPS)
     return q.astype(BF16), k.astype(BF16), kv[:, HD:].astype(BF16), bias[2:3]
 
 
@@ -388,7 +388,7 @@
         piece = folds.at[c, source_y(d), x, pl.ds(0, fold_rows)]
         quarters[d] = [
             send(piece, piece, sendq.at[d, dx], recvq.at[d, dx], at_x(dx))
-            for dx in near_first(nx)
+            for dx in reversed(near_first(nx))
         ]
 
     def arrived(d):
@@ -409,7 +409,7 @@
     inputs = [pick_clip(owner, 2 * ny, x_all, gram) for owner in (2 * y + 1 - c, e)]
     for name in ("qg", "kg"):
         loads[name].wait()
-    gain = qg_ref[...] * kg_ref[...] * (HD**-0.5 * math.log2(math.e))
+    gain = qg_ref[...] * kg_ref[...] * (HD**0.5 * math.log2(math.e))
 
     def project(heads):
         projected = []

time: 36.6 us -> 36.4 us (level)
  no operation moved by 1% of the time
where the time goes in v6:
time: 36.4 us; the launch traced here: 36.3 us
  Pallas kernels  35.5 us (98%)
  local copies, waits for them, and re-layouts  0.8 us (2%)
    pallas_call x1, Pallas kernels, on_device(): pl.pallas_call(functools.partial(whole_kernel, ny, nz, nx), out_shape=plt...  35.5 us
    unnamed x1, local copies, waits for them, and re-layouts  0.8 us

profile of v6, /device:TPU:1, one launch (start us, length us, event | category | flops | bytes accessed | tf_op | source)
XLA Modules:
  0.0 36.3 jit_solution(6363915630441470829)
XLA Ops:
  0.0 35.5 %encode_move_attend.1 = bf16[128,2048]{1,0:T(8,128)(2,1)S(1)} custom-call(s32[1,1,3]{2,1,0:T(1,128)} %dims_hbm.1, s32[1,1,2,2]{3,2,1,0:T(2,128)} %plan_hbm.1, bf16[1024,512]{1,0:T(8,128)(2,1)} %bitcast.8, bf16[432,512]{1,0:T(8,128)(2,1)} %bitcast.9, bf16[64,2048]{1,0:T(8,128)(2,1)} %embed_hbm.1, f32[1,2048]{1,0:T(1,128)} %bitcast.10, f32[1,2048]{1,0:T(1,128)} %bitcast.11, ...), custom_call_target="tpu_custom_call" | custom-call | tf_op jit(solution)/shard_map/encode_move_attend/pallas_call | solution.py:484
  35.5 0.8 %copy.12 = bf16[1,128,2048]{2,1,0:T(8,128)(2,1)} copy(bf16[1,128,2048]{2,1,0:T(8,128)(2,1)S(1)} %bitcast.7) | data formatting | bytes 1048576

commit v7 on v6

--- a/solution.py
+++ b/solution.py
@@ -335,9 +335,14 @@
     owner1 = (jnp.zeros((16, BLOCK), jnp.int32) + plan_ref[0, 0, 1, 0]).astype(F32)
     meta = jnp.where(row16 == 0, owner0, jnp.where(row16 == 1, owner1, count[:, :BLOCK]))
     x_all[e, 8] = meta.astype(BF16)
-    x_first = [
-        send(x_all.at[e], x_all.at[e], sendt.at[d], recvt.at[d], at_y(d)) for d in near_first(ny)
-    ]
+    def send_tokens(source, distance, step):
+        piece = x_all.at[source]
+        return send(piece, piece, sendt.at[distance], recvt.at[distance], at_y(step))
+
+    relay = ny == 8
+    x_first = {
+        d: send_tokens(e, d, d) for d in ((2, 6, 1, 7) if relay else near_first(ny))
+    }
     x_second = [send(x_all.at[e], x_all.at[e], sendu.at[0], recvu.at[0], sibling)]
 
     def finish(total):
@@ -355,17 +360,20 @@
     ]
     gram = gram_terms(embed_ref)
 
-    def pass_tokens(d, copy):
-        copy.wait_recv()
+    def pass_tokens(d):
+        x_first[d].wait_recv()
         source = mod(y - d + ny, ny) * 2 + c
+        if relay and d == 2:
+            x_first[3] = send_tokens(source, 3, 1)
+            x_first[4] = send_tokens(source, 4, 2)
+        if relay and d == 6:
+            x_first[5] = send_tokens(source, 5, 7)
         x_second.append(
             send(x_all.at[source], x_all.at[source], sendu.at[d], recvu.at[d], sibling)
         )
 
-    arriving = list(zip(near_first(ny), x_first))
-    early = len(arriving) // 2
-    for d, copy in arriving[:early]:
-        pass_tokens(d, copy)
+    for d in list(x_first):
+        pass_tokens(d)
     total = z_own[...].astype(F32)
     for copy in over_z:
         copy.wait_recv()
@@ -398,11 +406,11 @@
     crossed = []
     order = [0] + near_first(ny)
     spread(order[0])
-    for d, copy in arriving[early:]:
-        pass_tokens(d, copy)
+    for d in list(x_first)[4:]:
+        pass_tokens(d)
     for d in order[1:]:
         spread(d)
-    settle(over_x + over_z + list(over_y.values()) + x_first)
+    settle(over_x + over_z + list(over_y.values()) + list(x_first.values()))
     for copy in x_second:
         copy.wait_recv()
     settle(x_second)

time: 36.4 us -> 36.4 us (level)
  no operation moved by 1% of the time
where the time goes in v7:
time: 36.4 us; the launch traced here: 36.3 us
  Pallas kernels  35.5 us (98%)
  local copies, waits for them, and re-layouts  0.8 us (2%)
    pallas_call x1, Pallas kernels, on_device(): pl.pallas_call(functools.partial(whole_kernel, ny, nz, nx), out_shape=plt...  35.5 us
    unnamed x1, local copies, waits for them, and re-layouts  0.8 us

profile of v7, /device:TPU:1, one launch (start us, length us, event | category | flops | bytes accessed | tf_op | source)
XLA Modules:
  0.0 36.3 jit_solution(16165131242559546233)
XLA Ops:
  0.0 35.5 %encode_move_attend.1 = bf16[128,2048]{1,0:T(8,128)(2,1)S(1)} custom-call(s32[1,1,3]{2,1,0:T(1,128)} %dims_hbm.1, s32[1,1,2,2]{3,2,1,0:T(2,128)} %plan_hbm.1, bf16[1024,512]{1,0:T(8,128)(2,1)} %bitcast.8, bf16[432,512]{1,0:T(8,128)(2,1)} %bitcast.9, bf16[64,2048]{1,0:T(8,128)(2,1)} %embed_hbm.1, f32[1,2048]{1,0:T(1,128)} %bitcast.10, f32[1,2048]{1,0:T(1,128)} %bitcast.11, ...), custom_call_target="tpu_custom_call" | custom-call | tf_op jit(solution)/shard_map/encode_move_attend/pallas_call | solution.py:492
  35.5 0.8 %copy.12 = bf16[1,128,2048]{2,1,0:T(8,128)(2,1)} copy(bf16[1,128,2048]{2,1,0:T(8,128)(2,1)S(1)} %bitcast.7) | data formatting | bytes 1048576
